TPU v7x, 32 devices: a whole 2x2x4 slice. The times are simulated.
32 devices in a mesh: row: 8 (over y, x, core), col: 4 (over z).
Axes of the slice: x: 2, y: 2, z: 4, core: 2. Of those that a mesh axis runs over, the one named last changes fastest.
Arguments:
- activations: bfloat16 [384, 49, 512], P(('row', 'col'))
- pre_activation: bfloat16 [384, 49, 1024], P(('row', 'col')), may hold values from -6 to 6
- pooled_grad: float32 [384, 1024], P(('row', 'col')), may hold values from -300 to 300
- weights: bfloat16 [512, 1024], replicated, as said below
- master: float32 [512, 1024], P('row', 'col')
- velocity: float32 [512, 1024], P('row', 'col'), may hold values from -0.6 to 0.6
- bn_params: float32 [2, 1024], replicated, may hold values from 0.5 to 1.5
- bn_velocity: float32 [2, 1024], replicated, may hold values from -0.6 to 0.6
Outputs:
- input_grad: bfloat16 [384, 49, 512], P(('row', 'col'))
- new_master: float32 [512, 1024], P('row', 'col')
- new_velocity: float32 [512, 1024], P('row', 'col')
- new_weights: bfloat16 [512, 1024], replicated
- new_bn: float32 [2, 1024], replicated
- new_bn_velocity: float32 [2, 1024], replicated
Inputs may be any that keep to these rules, and one draw needn't show every extreme that they name: weights lies within one bfloat16 rounding of master, entry by entry.
All inputs are finite; a program needn't handle non-finite values.
Results may differ from a plain program's by a relative error of at most 0.0045.
The roundings to bfloat16 on the way count: a program that leaves them out, or rounds other values in their place, can miss the bound.
Values may be sent and summed in bfloat16 or wider, within the bound.
A program may use at most 64 MiB of HBM per device.

v0:
```python
import jax
import jax.numpy as jnp
from jax import lax
from jax.sharding import PartitionSpec as P

epsilon = 1e-05
trust_coef = 0.001
weight_decay = 0.0001
momentum = 0.9
learn_rate = 12.0


def body(
    activations, pre_activation, pooled_grad, weights, master, velocity, bn_params, bn_velocity
):
    images, positions, in_chan = activations.shape
    out_chan = weights.shape[1]
    row_count = images * positions
    n_row = lax.axis_size("row")
    n_col = lax.axis_size("col")
    group_element_count = row_count * n_col
    total_images = images * n_row * n_col
    norm_scale_weight = bn_params[0]
    flat_in = activations.reshape(row_count, in_chan)
    conv_low = jnp.dot(flat_in, weights, preferred_element_type=jnp.float32).astype(jnp.bfloat16)
    expand_conv_output = lax.optimization_barrier(conv_low).astype(jnp.float32)
    stats = lax.psum(
        (
            jnp.sum(expand_conv_output, axis=0),
            jnp.sum(expand_conv_output * expand_conv_output, axis=0),
        ),
        "col",
    )
    group_mean_value = stats[0] / group_element_count
    variance = stats[1] / group_element_count - group_mean_value * group_mean_value
    inverse_deviation = lax.rsqrt(variance + epsilon)
    upstream_all = jnp.broadcast_to(
        (pooled_grad / positions)[:, None, :], pre_activation.shape
    ).reshape(row_count, out_chan)
    incoming_gradient = jnp.where(
        pre_activation.reshape(row_count, out_chan) > 0, upstream_all, jnp.zeros_like(upstream_all)
    )
    normalized_input = (expand_conv_output - group_mean_value) * inverse_deviation
    local_up = jnp.sum(incoming_gradient, axis=0)
    local_upstream_normalized = jnp.sum(incoming_gradient * normalized_input, axis=0)
    group_totals_reduced = lax.psum((local_up, local_upstream_normalized), "col")
    expand_conv_gradient = (
        norm_scale_weight
        * inverse_deviation
        * (
            incoming_gradient
            - group_totals_reduced[0] / group_element_count
            - normalized_input * group_totals_reduced[1] / group_element_count
        )
    ).astype(jnp.bfloat16)
    back = lax.dot_general(
        expand_conv_gradient, weights, (((1,), (1,)), ((), ())), preferred_element_type=jnp.float32
    )
    input_grad = back.astype(jnp.bfloat16).reshape(images, positions, in_chan)
    row_part = lax.psum_scatter(
        lax.dot_general(
            flat_in,
            expand_conv_gradient,
            (((0,), (0,)), ((), ())),
            preferred_element_type=jnp.float32,
        ),
        "row",
        scatter_dimension=0,
        tiled=True,
    )
    grad_sum = lax.psum_scatter(row_part, "col", scatter_dimension=1, tiled=True)
    weight_grad = grad_sum * (1.0 / total_images)
    master_sq = jnp.sum(master * master)
    grad_sq = jnp.sum(weight_grad * weight_grad)
    bn_tot = lax.psum((group_totals_reduced[1], group_totals_reduced[0]), "row")
    norms = lax.psum((master_sq, grad_sq), ("row", "col"))
    upx_total, up_total = (bn_tot[0], bn_tot[1])
    master_total, grad_total = (norms[0], norms[1])
    wnorm = jnp.sqrt(master_total)
    gnorm = jnp.sqrt(grad_total)
    trust = trust_coef * wnorm / (gnorm + weight_decay * wnorm)
    new_velocity = momentum * velocity + learn_rate * trust * (weight_grad + weight_decay * master)
    new_master = master - new_velocity
    shard_low = new_master.astype(jnp.bfloat16)
    wide_rows = lax.all_gather(shard_low, "col", axis=1, tiled=True)
    new_weights = lax.all_gather(wide_rows, "row", axis=0, tiled=True)
    bn_grad = jnp.stack([upx_total, up_total]) * (1.0 / total_images)
    new_bn_velocity = momentum * bn_velocity + learn_rate * bn_grad
    new_bn = bn_params - new_bn_velocity
    return (input_grad, new_master, new_velocity, new_weights, new_bn, new_bn_velocity)


def solution(mesh):
    placed = (
        P(("row", "col"), None, None),
        P(("row", "col"), None, None),
        P(("row", "col"), None),
        P(),
        P("row", "col"),
        P("row", "col"),
        P(),
        P(),
    )
    return jax.shard_map(
        body,
        mesh=mesh,
        in_specs=placed,
        out_specs=(P(("row", "col"), None, None), P("row", "col"), P("row", "col"), P(), P(), P()),
        check_vma=False,
    )
```

profile of v0, /device:TPU:0, one launch (start us, length us, event | category | flops | bytes accessed | tf_op | source)
XLA Modules:
  0.0 202.4 jit_solution(17374673362903209525)
XLA Ops:
  7.2 0.0 copy-start
  7.2 0.0 copy-start.8
  7.2 0.0 copy-start.1
  7.2 0.0 reduce-scatter.7.cloned.1.call-start
  7.2 1.4 reshape.30
  8.7 0.0 copy-done
  8.7 0.0 copy-start.4
  8.7 1.8 convolution_convert_fusion
  10.5 0.0 copy-done.8
  10.6 0.0 copy-done.1
  10.6 2.0 %fusion.9 = (f32[1024]{0:T(1024)S(1)}, f32[12,49,1024]{2,1,0:T(8,128)}) fusion(f32[12,1024]{1,0:T(8,128)S(1)} %broadcast_multiply_fusion, bf16[12,49,1024]{2,1,0:T(8,128)(2,1)S(1)} %copy-done.1), kind=kLoop, calls=%fused_computation.16 | loop fusion | flops 1805312 | bytes 3665920 | tf_op jit(solution)/shard_map/reduce_sum | solution.py:44
  12.6 0.0 copy-done.4
  12.6 0.0 slice-start
  12.6 1.9 select_n.9
  14.5 1.6 convert_reduce_fusion
  16.1 13.7 %all-reduce.3 = (f32[1024]{0:T(1024)S(1)}, f32[1024]{0:T(1024)S(1)}) all-reduce(f32[1024]{0:T(1024)S(1)} %get-tuple-element.19, f32[1024]{0:T(1024)S(1)} %get-tuple-element.18), channel_id=1, replica_groups=mesh['row'=8,'col'=4] {'col'}, use_global_device_ids=true, to_apply=%region_1.0 | all-reduce | flops 2048 | bytes 16384 | tf_op jit(solution)/shard_map/psum | solution.py:27
  29.8 0.0 slice-done
  29.9 1.7 fusion.4
  31.6 8.5 %all-reduce.2 = (f32[1024]{0:T(1024)S(1)}, f32[1024]{0:T(1024)S(1)}) all-reduce(f32[1024]{0:T(1024)S(1)} %fusion.4, f32[1024]{0:T(1024)S(1)} %get-tuple-element.33), channel_id=1, replica_groups=mesh['row'=8,'col'=4] {'col'}, use_global_device_ids=true, to_apply=%region_7.8 | all-reduce | flops 2048 | bytes 16384 | tf_op jit(solution)/shard_map/psum | solution.py:46
  40.1 0.0 copy-start.5
  40.1 2.0 %fusion.8 = bf16[588,1024]{1,0:T(8,128)(2,1)S(1)} fusion(bf16[588,1024]{1,0:T(8,128)(2,1)} %convolution_convert_fusion, f32[588,1024]{1,0:T(8,128)S(1)} %select_n.9, f32[1024]{0:T(1024)S(1)} %get-tuple-element.24, f32[1024]{0:T(1024)S(1)} %get-tuple-element.36, f32[1024]{0:T(1024)S(1)} %get-tuple-element.37, f32[1024]{0:T(1024)S(1)} %broadcast_multiply_fusion.1, ...), kind=kLoop, calls=%fused_computation.12 | loop fusion | flops 5419008 | bytes 4837376 | tf_op jit(solution)/shard_map/convert_element_type | solution.py:55
  42.2 0.0 copy-start.2
  42.2 1.0 copy-done.2
  43.2 0.0 copy-done.5
  43.2 1.0 convolution_bitcast_fusion
  44.2 1.9 copy.26
  46.1 0.0 copy-start.6
  46.1 0.0 copy-start.7
  46.1 0.0 copy-start.3
  46.1 0.0 reduce-scatter.7.cloned.1.call-update
  46.1 0.0 reduce-scatter.5.cloned.1.call-start
  46.2 41.0 %reduce-scatter.7.cloned.1.call-done = f32[64,1024]{1,0:T(8,128)} async-done(((f32[512,1024]{1,0:T(8,128)}), f32[64,1024]{1,0:T(8,128)}) %reduce-scatter.7.cloned.1.call-update) | async-done | bytes 262160
  87.2 1.9 copy.27
  89.1 0.0 reduce-scatter.5.cloned.1.call-update
  89.1 0.0 all-gather.2.cloned.1.call-start
  89.2 0.0 copy-done.6
  89.2 0.1 copy.22
  89.3 0.6 multiply_reduce_fusion.1
  89.9 21.9 %reduce-scatter.5.cloned.1.call-done = f32[64,256]{0,1:T(8,128)} async-done(((f32[64,1024]{0,1:T(8,128)}), f32[64,256]{0,1:T(8,128)}) %reduce-scatter.5.cloned.1.call-update) | async-done | bytes 65552 | tf_op jit(solution)/shard_map/reduce_scatter | solution.py:71
  111.8 1.5 multiply_reduce_fusion
  113.3 0.0 copy-done.7
  113.3 0.1 copy.20
  113.4 38.8 %all-reduce = (f32[]{:T(128)}, f32[]{:T(128)}) all-reduce(f32[]{:T(128)} %multiply_reduce_fusion.1, f32[]{:T(128)} %multiply_reduce_fusion), channel_id=1, replica_groups=mesh['row'=8,'col'=4] {'row','col'}, use_global_device_ids=true, to_apply=%region_9.10 | all-reduce | flops 2 | bytes 16 | tf_op jit(solution)/shard_map/psum | solution.py:76
  153.7 1.0 fusion.14
  154.6 14.3 %all_gather.6 = bf16[64,1024]{0,1:T(8,128)(2,1)S(1)} all-gather(bf16[64,256]{0,1:T(8,128)(2,1)S(1)} %get-tuple-element.30), channel_id=1, replica_groups=mesh['row'=8,'col'=4] {'col'}, dimensions={1}, use_global_device_ids=true | all-gather | bytes 163840 | tf_op jit(solution)/shard_map/all_gather | solution.py:85
  169.0 0.8 copy.23
  169.7 0.0 all-gather.2.cloned.1.call-update
  169.8 0.0 copy-done.3
  169.8 0.0 copy-start.9
  169.8 0.0 copy-start.10
  169.8 0.8 convolution_convert_fusion.1
  170.6 1.0 reshape.31
  171.7 12.1 %all-reduce.1 = (f32[1,1024]{1,0:T(1,128)S(1)}, f32[1,1024]{1,0:T(1,128)S(1)}) all-reduce(f32[1,1024]{1,0:T(1,128)S(1)} %bitcast.13, f32[1,1024]{1,0:T(1,128)S(1)} %bitcast.14), channel_id=1, replica_groups=mesh['row'=8,'col'=4] {'row'}, use_global_device_ids=true, to_apply=%region_15.16 | all-reduce | flops 2048 | bytes 16384 | tf_op jit(solution)/shard_map/psum | solution.py:75
  183.8 0.0 copy-done.9
  183.8 0.0 copy-done.10
  183.8 0.6 fusion.12
  184.4 0.7 copy.24
  185.2 0.7 copy.25
  185.9 7.7 %all-gather.2.cloned.1.call-done = bf16[512,1024]{1,0:T(8,128)(2,1)} async-done(((bf16[64,1024]{1,0:T(8,128)(2,1)}), bf16[512,1024]{1,0:T(8,128)(2,1)}) %all-gather.2.cloned.1.call-update) | async-done | bytes 1048592 | tf_op jit(solution)/shard_map/all_gather | solution.py:86
  193.6 2.3 %copy.29 = bf16[512,1024]{1,0:T(8,128)(2,1)} copy(bf16[512,1024]{1,0:T(8,128)(2,1)} %all-gather.2.cloned.1.call-done) | data formatting | bytes 2097152
  (3 shorter events, 0.0 us)
Async XLA Ops:
  7.2 1.5 copy-start
  7.2 3.4 %copy-start.8 = (f32[12,1024]{1,0:T(8,128)S(1)}, f32[12,1024]{1,0:T(8,128)}, u32[]{:S(2)}) copy-start(f32[12,1024]{1,0:T(8,128)} %param.10) | copy-start | bytes 147460
  7.2 3.4 %copy-start.1 = (bf16[12,49,1024]{2,1,0:T(8,128)(2,1)S(1)}, bf16[12,49,1024]{2,1,0:T(8,128)(2,1)}, u32[]{:S(2)}) copy-start(bf16[12,49,1024]{2,1,0:T(8,128)(2,1)} %param.9) | copy-start | bytes 3612676
  7.2 80.0 %reduce-scatter.7.cloned.1.call-start = ((), (), s32[]{:S(2)}) async-start(), calls=%async_computation.4 | async-start | bytes 2359296
  8.7 3.9 %copy-start.4 = (bf16[588,512]{1,0:T(8,128)(2,1)}, bf16[588,512]{1,0:T(8,128)(2,1)S(1)}, u32[]{:S(2)}) copy-start(bf16[588,512]{1,0:T(8,128)(2,1)S(1)} %reshape.30) | copy-start | bytes 1806340
  12.6 17.2 %slice-start = ((f32[2,1024]{1,0:T(2,128)}), f32[1,1024]{1,0:T(1,128)S(1)}, s32[]{:S(2)}) async-start(f32[2,1024]{1,0:T(2,128)} %param.14), calls=%async_computation.5 | async-start | bytes 8192 | tf_op jit(solution)/shard_map/slice | solution.py:23
  40.1 3.1 %copy-start.5 = (bf16[588,512]{1,0:T(8,128)(2,1)S(1)}, bf16[588,512]{1,0:T(8,128)(2,1)}, u32[]{:S(2)}) copy-start(bf16[588,512]{1,0:T(8,128)(2,1)} %copy-done.4) | copy-start | bytes 1806340
  42.2 1.0 copy-start.2
  46.1 43.1 %copy-start.6 = (f32[64,256]{1,0:T(8,128)S(1)}, f32[64,256]{1,0:T(8,128)}, u32[]{:S(2)}) copy-start(f32[64,256]{1,0:T(8,128)} %param.12) | copy-start | bytes 196612
  46.1 67.2 %copy-start.7 = (f32[64,256]{1,0:T(8,128)S(1)}, f32[64,256]{1,0:T(8,128)}, u32[]{:S(2)}) copy-start(f32[64,256]{1,0:T(8,128)} %param.13) | copy-start | bytes 196612
  46.1 123.7 %copy-start.3 = (bf16[588,1024]{1,0:T(8,128)(2,1)S(1)}, bf16[588,1024]{1,0:T(8,128)(2,1)}, u32[]{:S(2)}) copy-start(bf16[588,1024]{1,0:T(8,128)(2,1)} %copy-done.2) | copy-start | bytes 3612676
  46.1 65.6 %reduce-scatter.5.cloned.1.call-start = ((), (), s32[]{:S(2)}) async-start(), calls=%async_computation.2 | async-start | bytes 655360 | tf_op jit(solution)/shard_map/reduce_scatter | solution.py:71
  89.1 104.5 %all-gather.2.cloned.1.call-start = ((), (), s32[]{:S(2)}) async-start(), calls=%async_computation.3 | async-start | bytes 1179648 | tf_op jit(solution)/shard_map/all_gather | solution.py:86
  169.8 14.0 %copy-start.9 = (f32[2,1024]{1,0:T(2,128)S(1)}, f32[2,1024]{1,0:T(2,128)}, u32[]{:S(2)}) copy-start(f32[2,1024]{1,0:T(2,128)} %param.14) | copy-start | bytes 24580
  169.8 14.0 %copy-start.10 = (f32[2,1024]{1,0:T(2,128)S(1)}, f32[2,1024]{1,0:T(2,128)}, u32[]{:S(2)}) copy-start(f32[2,1024]{1,0:T(2,128)} %param.15) | copy-start | bytes 24580
Sparse Core Ops, SparseCore 0:
  46.2 40.8 reduce-scatter.6
  90.1 21.6 reduce-scatter.4
  169.9 23.6 all-gather.1
where the time goes:
time: 203 us; the launch traced here: 202 us
  blocking collectives  87.5 us (43%)
  waiting for transfers between devices  70.6 us (35%)
  between operations  15.4 us (8%)
  local copies, waits for them, and re-layouts  13.9 us (7%)
  other arithmetic  11.2 us (6%)
  matrix products  3.67 us (2%)
    unnamed x4, waiting for transfers between devices  41 us
    psum x1, blocking collectives, body(): norms = lax.psum((master_sq, grad_sq), ('row', 'col'))  38.8 us
    reduce_scatter x1, waiting for transfers between devices, body(): lax.psum_scatter(row_part, 'col', scatter_dimension=1, tiled=True)  21.9 us
    all_gather x1, blocking collectives, body(): wide_rows = lax.all_gather(shard_low, 'col', axis=1, tiled=True)  14.3 us
    psum x1, blocking collectives, body(): lax.psum((jnp.sum(expand_conv_output, axis=0), jnp.sum(expand_conv_output...  13.7 us
    psum x1, blocking collectives, body(): bn_tot = lax.psum((group_totals_reduced[1], group_totals_reduced[0]), 'row')  12.1 us
    unnamed x29, local copies, waits for them, and re-layouts  8.78 us
    psum x1, blocking collectives, body(): lax.psum((local_up, local_upstream_normalized), 'col')  8.51 us
  transfers between devices with their start and end apart: 3, of which 3 were waited for; matrix products, arithmetic and copies ran while one was open for 2% of the time, Pallas kernels for 0%

commit v1 on v0

--- a/solution.py
+++ b/solution.py
@@ -1,6 +1,10 @@
+import functools
+
 import jax
 import jax.numpy as jnp
 from jax import lax
+from jax.experimental import pallas as pl
+from jax.experimental.pallas import tpu as pltpu
 from jax.sharding import PartitionSpec as P
 
 epsilon = 1e-05
@@ -90,6 +94,386 @@
     return (input_grad, new_master, new_velocity, new_weights, new_bn, new_bn_velocity)
 
 
+MESH = pl.DeviceIdType.MESH
+PAD = 64
+CW = 256
+
+
+def flip(value, bit):
+    return lax.rem(value + bit, 2)
+
+
+def kernel(
+    act_hbm, pre_hbm, pool_ref, w_hbm, master_ref, velocity_ref, bn_ref, bnv_ref,
+    ig_hbm, nm_ref, nv_ref, nw_hbm, nbn_ref, nbv_ref,
+    act, pre, w, a_s, at, conv, cg, poolg, ig, wout,
+    st_s, st_r, bn_s, bn_r, sa, ra, own, sb, rb, sc, rc, sd, rd, acc, n1s, n1r, n2s, n2r,
+    in_sem, out_sem, st_ss, st_rs, bn_ss, bn_rs, a_ss, a_rs, b_ss, b_rs, c_ss, c_rs, d_ss, d_rs,
+    n1_ss, n1_rs, n2_ss, n2_rs, z_ss, z_rs, f_ss, f_rs, g_ss, g_rs, k_ss, k_rs,
+):
+    images, positions, in_chan = act.shape
+    out_chan = w.shape[1]
+    n_row, n_col = 8, 4
+    rblk, cblk = in_chan // n_row, out_chan // n_col
+    half = out_chan // 2
+    device_count = images * positions
+    count = device_count * n_col
+    total_images = images * n_row * n_col
+    r, z = lax.axis_index("row"), lax.axis_index("col")
+    k, x, y = lax.rem(r, 2), lax.rem(r // 2, 2), r // 4
+
+    def row_of(yy, xx, kk):
+        return 4 * yy + 2 * xx + kk
+
+    def row_peer(j):
+        return row_of(flip(y, j // 4), flip(x, (j // 2) % 2), flip(k, j % 2))
+
+    def col_peer(i):
+        return 2 * flip(z // 2, i // 2) + flip(lax.rem(z, 2), i % 2)
+
+    def send(src, dst, ss, rs, row, col):
+        copy = pltpu.make_async_remote_copy(
+            src_ref=src, dst_ref=dst, send_sem=ss, recv_sem=rs,
+            device_id=(row, col), device_id_type=MESH,
+        )
+        copy.start()
+        return copy
+
+    barrier = pltpu.get_barrier_semaphore()
+    for j in range(1, n_row):
+        pl.semaphore_signal(barrier, inc=1, device_id=(row_peer(j), z), device_id_type=MESH)
+    for i in range(1, n_col):
+        pl.semaphore_signal(barrier, inc=1, device_id=(r, col_peer(i)), device_id_type=MESH)
+
+    loads = [
+        pltpu.make_async_copy(src, dst, in_sem.at[n])
+        for n, (src, dst) in enumerate(((act_hbm, act), (w_hbm, w), (pre_hbm, pre)))
+    ]
+    for load in loads:
+        load.start()
+
+    cg[...] = jnp.zeros_like(cg)
+    a_s[...] = jnp.zeros_like(a_s)
+    poolg[...] = pool_ref[...] / positions
+    st_s[...] = jnp.zeros_like(st_s)
+    msq = jnp.sum(master_ref[...] * master_ref[...], axis=0, keepdims=True)
+    m_part = functools.reduce(lambda p, q: p + q, [msq[:, c : c + 128] for c in range(0, cblk, 128)])
+
+    loads[0].wait()
+    for im in range(images):
+        a_s[PAD * im : PAD * im + positions, :] = act[im]
+    loads[1].wait()
+    loads[2].wait()
+    for c in range(0, out_chan, CW):
+        cols = slice(c, c + CW)
+        low = jnp.dot(a_s[...], w[:, cols], preferred_element_type=jnp.float32).astype(jnp.bfloat16)
+        conv[:, cols] = low
+        wide = low.astype(jnp.float32)
+        total = jnp.sum(wide, axis=0, keepdims=True)
+        mean = total / device_count
+        st_s[0:1, cols] = total
+        st_s[1:2, cols] = jnp.sum(wide * wide, axis=0, keepdims=True)
+        up_sum = jnp.zeros((1, CW), jnp.float32)
+        upx_sum = jnp.zeros((1, CW), jnp.float32)
+        for im in range(images):
+            rows = conv[PAD * im : PAD * im + positions, cols].astype(jnp.float32)
+            keep = pre[im, :, cols].astype(jnp.float32) > 0
+            pooled = poolg[im : im + 1, cols]
+            up_sum += pooled * jnp.sum(jnp.where(keep, 1.0, 0.0), axis=0, keepdims=True)
+            upx_sum += pooled * jnp.sum(jnp.where(keep, rows - mean, 0.0), axis=0, keepdims=True)
+        st_s[2:3, cols] = up_sum
+        st_s[3:4, cols] = upx_sum
+
+    pl.semaphore_wait(barrier, n_row + n_col - 2)
+    sends = []
+    st = [
+        send(st_s, st_r.at[i - 1], st_ss.at[i - 1], st_rs.at[i - 1], r, col_peer(i))
+        for i in range(1, n_col)
+    ]
+    turned = a_s[...].T
+    for q in range(n_row):
+        at[q % 2, (q // 2) * rblk : (q // 2 + 1) * rblk, :] = turned[q * rblk : (q + 1) * rblk, :]
+    for copy in st:
+        copy.wait_recv()
+    parts = [st_s[...]] + [st_r[i] for i in range(n_col - 1)]
+    mu = (parts[0][0:1] + parts[1][0:1] + parts[2][0:1] + parts[3][0:1]) / count
+    square = parts[0][1:2] + parts[1][1:2] + parts[2][1:2] + parts[3][1:2]
+    su = parts[0][2:3] + parts[1][2:3] + parts[2][2:3] + parts[3][2:3]
+    rstd = lax.rsqrt(square / count - mu * mu + epsilon)
+    sx = jnp.zeros_like(mu)
+    for part in parts:
+        sx += part[3:4] + (part[0:1] / device_count - mu) * part[2:3]
+    sx = sx * rstd
+    bn_s[0:1, :] = sx
+    bn_s[1:2, :] = su
+    bn = [
+        send(bn_s, bn_r.at[j - 1], bn_ss.at[j - 1], bn_rs.at[j - 1], row_peer(j), z)
+        for j in range(1, n_row)
+    ]
+    scale = bn_ref[0:1, :] * rstd
+    shift = scale * su / count
+    slope = scale * rstd * sx / count
+
+    def grad_columns(c):
+        cols = slice(c, c + CW)
+        for im in range(images):
+            span = slice(PAD * im, PAD * im + positions)
+            rows = conv[span, cols].astype(jnp.float32)
+            keep = pre[im, :, cols].astype(jnp.float32) > 0
+            up = jnp.where(keep, scale[:, cols] * poolg[im : im + 1, cols], 0.0)
+            grad = up - shift[:, cols] - slope[:, cols] * (rows - mu[:, cols])
+            cg[span, cols] = grad.astype(jnp.bfloat16)
+
+    core = []
+    for h in range(2):
+        for c in range(h * half, (h + 1) * half, CW):
+            grad_columns(c)
+        block = jnp.dot(at[1 - k], cg[:, h * half : (h + 1) * half], preferred_element_type=jnp.float32)
+        sa[h] = block.reshape(4, rblk, half)
+        core.append(send(sa.at[h], ra.at[h], a_ss.at[h], a_rs.at[h], row_of(y, x, 1 - k), z))
+    for h in range(2):
+        block = jnp.dot(at[k], cg[:, h * half : (h + 1) * half], preferred_element_type=jnp.float32)
+        own[h] = block.reshape(4, rblk, half)
+
+    x_peer, y_peer = row_of(y, 1 - x, k), row_of(1 - y, x, k)
+    first, second = (x_peer, y_peer), (y_peer, x_peer)
+
+    def keep_q(h, j):
+        return 2 * j + x if h == 0 else 2 * y + j
+
+    def send_q(h, j):
+        return 2 * j + 1 - x if h == 0 else 2 * (1 - y) + j
+
+    step_b = []
+    for h in range(2):
+        core[h].wait_recv()
+        for j in range(2):
+            q = send_q(h, j)
+            sb[h, j] = (own[h, q] + ra[h, q]).astype(jnp.bfloat16)
+        step_b.append(send(sb.at[h], rb.at[h], b_ss.at[h], b_rs.at[h], first[h], z))
+
+    def input_rows(lo, hi):
+        back = lax.dot_general(
+            cg[PAD * lo : PAD * hi, :], w[...], (((1,), (1,)), ((), ())),
+            preferred_element_type=jnp.float32,
+        ).astype(jnp.bfloat16)
+        for im in range(lo, hi):
+            ig[im] = back[PAD * (im - lo) : PAD * (im - lo) + positions, :]
+
+    input_rows(0, images // 2)
+    step_c = []
+    for h in range(2):
+        step_b[h].wait_recv()
+        near = 1 - y if h == 0 else 1 - x
+        q = keep_q(h, near)
+        sc[h] = (own[h, q] + ra[h, q] + rb[h, near].astype(jnp.float32)).astype(jnp.bfloat16)
+        step_c.append(send(sc.at[h], rc.at[h], c_ss.at[h], c_rs.at[h], second[h], z))
+    input_rows(images // 2, images)
+    out_copies = [pltpu.make_async_copy(ig, ig_hbm, out_sem.at[0])]
+    out_copies[0].start()
+    for h in range(2):
+        step_c[h].wait_recv()
+        mine = y if h == 0 else x
+        q = 2 * y + x
+        done = own[h, q] + ra[h, q] + rb[h, mine].astype(jnp.float32) + rc[h].astype(jnp.float32)
+        acc[2 * h] = done[:, :cblk]
+        acc[2 * h + 1] = done[:, cblk:]
+    step_d = []
+    for i in range(1, n_col):
+        sd[i - 1] = acc[col_peer(i)].astype(jnp.bfloat16)
+        step_d.append(send(sd.at[i - 1], rd.at[i - 1], d_ss.at[i - 1], d_rs.at[i - 1], r, col_peer(i)))
+    grad = acc[z]
+    for i in range(n_col - 1):
+        step_d[i].wait_recv()
+        grad += rd[i].astype(jnp.float32)
+    grad = grad * (1.0 / total_images)
+
+    gsq = jnp.sum(grad * grad, axis=0, keepdims=True)
+    g_part = functools.reduce(lambda p, q: p + q, [gsq[:, c : c + 128] for c in range(0, cblk, 128)])
+    n1s[...] = jnp.zeros_like(n1s)
+    n1s[0:1, :] = g_part
+    n1s[1:2, :] = m_part
+    norm1 = [
+        send(n1s, n1r.at[j - 1], n1_ss.at[j - 1], n1_rs.at[j - 1], row_peer(j), z)
+        for j in range(1, n_row)
+    ]
+    norm = n1s[...]
+    for j in range(n_row - 1):
+        norm1[j].wait_recv()
+        norm += n1r[j]
+    n2s[...] = norm
+    norm2 = [
+        send(n2s, n2r.at[i - 1], n2_ss.at[i - 1], n2_rs.at[i - 1], r, col_peer(i))
+        for i in range(1, n_col)
+    ]
+    for i in range(n_col - 1):
+        norm2[i].wait_recv()
+        norm += n2r[i]
+    gnorm = jnp.sqrt(jnp.sum(norm[0:1, :], axis=1, keepdims=True))
+    wnorm = jnp.sqrt(jnp.sum(norm[1:2, :], axis=1, keepdims=True))
+    trust = trust_coef * wnorm / (gnorm + weight_decay * wnorm)
+    weights_now = master_ref[...]
+    new_velocity = momentum * velocity_ref[...] + learn_rate * trust * (grad + weight_decay * weights_now)
+    new_master = weights_now - new_velocity
+    nv_ref[...] = new_velocity
+    nm_ref[...] = new_master
+
+    def block(row, p):
+        rows = pl.ds(pl.multiple_of(row * rblk, rblk), rblk)
+        return wout.at[rows, pl.ds(pl.multiple_of(p * cblk, cblk), cblk)]
+
+    def order(i):
+        return col_peer(i)
+
+    wout[pl.ds(pl.multiple_of(r * rblk, rblk), rblk), pl.ds(pl.multiple_of(z * cblk, cblk), cblk)] = (
+        new_master.astype(jnp.bfloat16)
+    )
+    zs = [
+        send(block(r, z), block(r, z), z_ss.at[i - 1], z_rs.at[i - 1], r, col_peer(i))
+        for i in range(1, n_col)
+    ]
+    sibling = row_of(y, x, 1 - k)
+
+    def near_row(p):
+        h = p // 2
+        return row_of(flip(y, 1 - h), flip(x, h), k)
+
+    def far_row(p):
+        h = p // 2
+        return row_of(flip(y, h), flip(x, 1 - h), k)
+
+    def to_sibling(row, p, slot):
+        sends.append(send(block(row, p), block(row, p), k_ss.at[slot], k_rs.at[slot], sibling, z))
+
+    near_sends, far_sends = [], []
+    for i in range(n_col):
+        p = order(i)
+        if i > 0:
+            src = block(r, p)
+            pltpu.make_async_remote_copy(
+                src_ref=src, dst_ref=src, send_sem=z_ss.at[i - 1], recv_sem=z_rs.at[i - 1],
+                device_id=(r, p), device_id_type=MESH,
+            ).wait_recv()
+        near_sends.append(send(block(r, p), block(r, p), f_ss.at[i], f_rs.at[i], near_row(p), z))
+        far_sends.append(send(block(r, p), block(r, p), g_ss.at[i], g_rs.at[i], far_row(p), z))
+        to_sibling(r, p, i)
+
+    def arrived(row, p, ss, rs, source):
+        ref = block(row, p)
+        pltpu.make_async_remote_copy(
+            src_ref=ref, dst_ref=ref, send_sem=ss, recv_sem=rs, device_id=(source, z), device_id_type=MESH
+        ).wait_recv()
+
+    for i in range(n_col):
+        p = order(i)
+        got = near_row(p)
+        arrived(got, p, f_ss.at[i], f_rs.at[i], got)
+        far_sends.append(
+            send(block(got, p), block(got, p), g_ss.at[4 + i], g_rs.at[4 + i], far_row(p), z)
+        )
+        to_sibling(got, p, 4 + i)
+    diagonal = row_of(1 - y, 1 - x, k)
+    for i in range(n_col):
+        p = order(i)
+        source = far_row(p)
+        arrived(source, p, g_ss.at[i], g_rs.at[i], source)
+        to_sibling(source, p, 8 + i)
+    for i in range(n_col):
+        p = order(i)
+        arrived(diagonal, p, g_ss.at[4 + i], g_rs.at[4 + i], far_row(p))
+        to_sibling(diagonal, p, 12 + i)
+
+    sums = bn_s[...]
+    for j in range(n_row - 1):
+        bn[j].wait_recv()
+        sums += bn_r[j]
+    new_bnv = momentum * bnv_ref[...] + learn_rate * (sums * (1.0 / total_images))
+    nbv_ref[...] = new_bnv
+    nbn_ref[...] = bn_ref[...] - new_bnv
+
+    for i in range(n_col):
+        p = order(i)
+        rows = (r, near_row(p), far_row(p), diagonal)
+        for n in range(4):
+            arrived(rows[n] + 1 - 2 * k, p, k_ss.at[4 * n + i], k_rs.at[4 * n + i], sibling)
+    out_copies.append(pltpu.make_async_copy(wout, nw_hbm, out_sem.at[1]))
+    out_copies[1].start()
+    for copy in st + bn + core + step_b + step_c + step_d + norm1 + norm2 + zs + near_sends + far_sends + sends:
+        copy.wait_send()
+    for copy in out_copies:
+        copy.wait()
+
+
+def fused(activations, pre_activation, pooled_grad, weights, master, velocity, bn_params, bn_velocity):
+    images, positions, in_chan = activations.shape
+    out_chan = weights.shape[1]
+    rows = images * PAD
+    rblk, cblk = master.shape
+    half = out_chan // 2
+    f32, bf16 = jnp.float32, jnp.bfloat16
+    vmem = pl.BlockSpec(memory_space=pltpu.VMEM)
+    hbm = pl.BlockSpec(memory_space=pl.ANY)
+    dma = pltpu.SemaphoreType.DMA
+    pairs = (3, 7, 2, 2, 2, 3, 7, 3, 3, 4, 8, 16)
+    flops = 6 * images * positions * in_chan * out_chan
+    return pl.pallas_call(
+        kernel,
+        out_shape=(
+            jax.ShapeDtypeStruct(activations.shape, bf16),
+            jax.ShapeDtypeStruct(master.shape, f32),
+            jax.ShapeDtypeStruct(master.shape, f32),
+            jax.ShapeDtypeStruct(weights.shape, bf16),
+            jax.ShapeDtypeStruct(bn_params.shape, f32),
+            jax.ShapeDtypeStruct(bn_params.shape, f32),
+        ),
+        in_specs=[hbm, hbm, vmem, hbm, vmem, vmem, vmem, vmem],
+        out_specs=(hbm, vmem, vmem, hbm, vmem, vmem),
+        scratch_shapes=[
+            pltpu.VMEM(activations.shape, bf16),
+            pltpu.VMEM(pre_activation.shape, bf16),
+            pltpu.VMEM(weights.shape, bf16),
+            pltpu.VMEM((rows, in_chan), bf16),
+            pltpu.VMEM((2, in_chan // 2, rows), bf16),
+            pltpu.VMEM((rows, out_chan), bf16),
+            pltpu.VMEM((rows, out_chan), bf16),
+            pltpu.VMEM(pooled_grad.shape, f32),
+            pltpu.VMEM(activations.shape, bf16),
+            pltpu.VMEM(weights.shape, bf16),
+            pltpu.VMEM((4, out_chan), f32),
+            pltpu.VMEM((3, 4, out_chan), f32),
+            pltpu.VMEM((2, out_chan), f32),
+            pltpu.VMEM((7, 2, out_chan), f32),
+            pltpu.VMEM((2, 4, rblk, half), f32),
+            pltpu.VMEM((2, 4, rblk, half), f32),
+            pltpu.VMEM((2, 4, rblk, half), f32),
+            pltpu.VMEM((2, 2, rblk, half), bf16),
+            pltpu.VMEM((2, 2, rblk, half), bf16),
+            pltpu.VMEM((2, rblk, half), bf16),
+            pltpu.VMEM((2, rblk, half), bf16),
+            pltpu.VMEM((3, rblk, cblk), bf16),
+            pltpu.VMEM((3, rblk, cblk), bf16),
+            pltpu.VMEM((4, rblk, cblk), f32),
+            pltpu.VMEM((8, 128), f32),
+            pltpu.VMEM((7, 8, 128), f32),
+            pltpu.VMEM((8, 128), f32),
+            pltpu.VMEM((3, 8, 128), f32),
+            dma((3,)),
+            dma((2,)),
+        ]
+        + [dma((n,)) for n in pairs for _ in range(2)],
+        compiler_params=pltpu.CompilerParams(
+            collective_id=0, has_side_effects=True, vmem_limit_bytes=48 * 1024 * 1024
+        ),
+        cost_estimate=pl.CostEstimate(flops=flops, bytes_accessed=8 * 1024 * 1024, transcendentals=0),
+    )(activations, pre_activation, pooled_grad, weights, master, velocity, bn_params, bn_velocity)
+
+
+def pick(mesh):
+    if mesh.shape["row"] == 8 and mesh.shape["col"] == 4:
+        return fused
+    return body
+
+
 def solution(mesh):
     placed = (
         P(("row", "col"), None, None),
@@ -102,7 +486,7 @@
         P(),
     )
     return jax.shard_map(
-        body,
+        pick(mesh),
         mesh=mesh,
         in_specs=placed,
         out_specs=(P(("row", "col"), None, None), P("row", "col"), P("row", "col"), P(), P(), P()),

time: 203 us -> 57.7 us (0.28)
  blocking collectives: 87.5 us -> 0 us
  waiting for transfers between devices: 70.6 us -> 0 us
  Pallas kernels: 0 us -> 44.7 us
  between operations: 15.4 us -> 0.66 us
  other arithmetic: 11.2 us -> 0 us
  matrix products: 3.67 us -> 0 us
  local copies, waits for them, and re-layouts: 13.9 us -> 11.8 us
    psum x4 -> x0, blocking collectives: 73.2 us -> none  [the longest x1 38.8 us: body(): norms = lax.psum((master_sq, grad_sq), ('row', 'col'))]
    pallas_call x0 -> x1, Pallas kernels: none -> 44.7 us  [fused(): pl.pallas_call(kernel, out_shape=(jax.ShapeDtypeStruct(activations.shape,...]
    unnamed x4 -> x0, waiting for transfers between devices: 41 us -> none
    reduce_scatter x1 -> x0, waiting for transfers between devices: 21.9 us -> none  [body(): lax.psum_scatter(row_part, 'col', scatter_dimension=1, tiled=True)]
    all_gather x1 -> x0, blocking collectives: 14.3 us -> none  [body(): wide_rows = lax.all_gather(shard_low, 'col', axis=1, tiled=True)]
    all_gather x1 -> x0, waiting for transfers between devices: 7.74 us -> none  [body(): new_weights = lax.all_gather(wide_rows, 'row', axis=0, tiled=True)]
    reduce_sum x5 -> x0, other arithmetic: 7.57 us -> none  [the longest x1 2.03 us: body(): local_up = jnp.sum(incoming_gradient, axis=0)]
    dot_general x3 -> x0, matrix products: 3.67 us -> none  [the longest x1 1.83 us: body(): jnp.dot(flat_in, weights, preferred_element_type=jnp.float32)]
  transfers between devices with their start and end apart: 3 -> 0, of which waited for: 3 -> 0; matrix products, arithmetic and copies ran while one was open for 2% -> 0% of each run, Pallas kernels for 0% -> 0%
where the time goes in v1:
time: 57.7 us; the launch traced here: 57.2 us
  Pallas kernels  44.7 us (77%)
  local copies, waits for them, and re-layouts  11.8 us (20%)
  between operations  0.66 us (1%)
    pallas_call x1, Pallas kernels, fused(): pl.pallas_call(kernel, out_shape=(jax.ShapeDtypeStruct(activations.shape,...  44.7 us
    unnamed x22, local copies, waits for them, and re-layouts  11.8 us

profile of v1, /device:TPU:0, one launch (start us, length us, event | category | flops | bytes accessed | tf_op | source)
XLA Modules:
  0.0 57.2 jit_solution(6215171997792290728)
XLA Ops:
  0.6 0.0 copy-start
  0.6 1.3 %copy-done = bf16[12,49,1024]{2,1,0:T(8,128)(2,1)S(1)} copy-done((bf16[12,49,1024]{2,1,0:T(8,128)(2,1)S(1)}, bf16[12,49,1024]{2,1,0:T(8,128)(2,1)}, u32[]{:S(2)}) %copy-start) | copy-done | bytes 1204248
  2.0 0.0 copy-start.1
  2.0 1.2 %copy-done.1 = bf16[512,1024]{1,0:T(8,128)(2,1)S(1)} copy-done((bf16[512,1024]{1,0:T(8,128)(2,1)S(1)}, bf16[512,1024]{1,0:T(8,128)(2,1)}, u32[]{:S(2)}) %copy-start.1) | copy-done | bytes 1048600
  3.2 0.0 copy-start.2
  3.2 1.1 %copy-done.2 = bf16[12,49,512]{2,1,0:T(8,128)(2,1)S(1)} copy-done((bf16[12,49,512]{2,1,0:T(8,128)(2,1)S(1)}, bf16[12,49,512]{2,1,0:T(8,128)(2,1)}, u32[]{:S(2)}) %copy-start.2) | copy-done | bytes 602136
  4.3 0.0 copy-start.3
  4.3 0.8 %copy-done.3 = f32[12,1024]{1,0:T(8,128)S(1)} copy-done((f32[12,1024]{1,0:T(8,128)S(1)}, f32[12,1024]{1,0:T(8,128)}, u32[]{:S(2)}) %copy-start.3) | copy-done | bytes 49176
  5.1 0.0 copy-start.4
  5.1 0.8 %copy-done.4 = f32[64,256]{1,0:T(8,128)S(1)} copy-done((f32[64,256]{1,0:T(8,128)S(1)}, f32[64,256]{1,0:T(8,128)}, u32[]{:S(2)}) %copy-start.4) | copy-done | bytes 65560
  6.0 0.0 copy-start.5
  6.0 0.8 %copy-done.5 = f32[64,256]{1,0:T(8,128)S(1)} copy-done((f32[64,256]{1,0:T(8,128)S(1)}, f32[64,256]{1,0:T(8,128)}, u32[]{:S(2)}) %copy-start.5) | copy-done | bytes 65560
  6.8 0.0 copy-start.6
  6.8 0.7 %copy-done.6 = f32[2,1024]{1,0:T(2,128)S(1)} copy-done((f32[2,1024]{1,0:T(2,128)S(1)}, f32[2,1024]{1,0:T(2,128)}, u32[]{:S(2)}) %copy-start.6) | copy-done | bytes 8216
  7.5 0.0 copy-start.7
  7.5 0.7 %copy-done.7 = f32[2,1024]{1,0:T(2,128)S(1)} copy-done((f32[2,1024]{1,0:T(2,128)S(1)}, f32[2,1024]{1,0:T(2,128)}, u32[]{:S(2)}) %copy-start.7) | copy-done | bytes 8216
  8.2 44.7 %shard_map.127 = (bf16[12,49,512]{2,1,0:T(8,128)(2,1)S(1)}, f32[64,256]{1,0:T(8,128)S(1)}, f32[64,256]{1,0:T(8,128)S(1)}, bf16[512,1024]{1,0:T(8,128)(2,1)S(1)},...) custom-call(bf16[12,49,512]{2,1,0:T(8,128)(2,1)S(1)} %copy-done.2, bf16[12,49,1024]{2,1,0:T(8,128)(2,1)S(1)} %copy-done, ...), custom_call_target="tpu_custom_call" | custom-call | flops 1849688064 | bytes 8388608 | tf_op jit(solution)/shard_map/pallas_call | solution.py:419
  52.9 0.8 %copy.20 = bf16[12,49,512]{2,1,0:T(8,128)(2,1)} copy(bf16[12,49,512]{2,1,0:T(8,128)(2,1)S(1)} %get-tuple-element.12) | data formatting | bytes 1204224
  53.7 0.6 %copy.21 = f32[64,256]{1,0:T(8,128)} copy(f32[64,256]{1,0:T(8,128)S(1)} %get-tuple-element.13) | data formatting | bytes 131072
  54.4 0.6 %copy.22 = f32[64,256]{1,0:T(8,128)} copy(f32[64,256]{1,0:T(8,128)S(1)} %get-tuple-element.14) | data formatting | bytes 131072
  55.0 1.0 %copy.23 = bf16[512,1024]{1,0:T(8,128)(2,1)} copy(bf16[512,1024]{1,0:T(8,128)(2,1)S(1)} %get-tuple-element.15) | data formatting | bytes 2097152
  56.0 0.6 %copy.24 = f32[2,1024]{1,0:T(2,128)} copy(f32[2,1024]{1,0:T(2,128)S(1)} %get-tuple-element.16) | data formatting | bytes 16384
  56.6 0.6 %copy.25 = f32[2,1024]{1,0:T(2,128)} copy(f32[2,1024]{1,0:T(2,128)S(1)} %get-tuple-element.17) | data formatting | bytes 16384
Async XLA Ops:
  0.6 1.3 %copy-start = (bf16[12,49,1024]{2,1,0:T(8,128)(2,1)S(1)}, bf16[12,49,1024]{2,1,0:T(8,128)(2,1)}, u32[]{:S(2)}) copy-start(bf16[12,49,1024]{2,1,0:T(8,128)(2,1)} %pre_hbm.1) | copy-start | bytes 3612676
  2.0 1.2 %copy-start.1 = (bf16[512,1024]{1,0:T(8,128)(2,1)S(1)}, bf16[512,1024]{1,0:T(8,128)(2,1)}, u32[]{:S(2)}) copy-start(bf16[512,1024]{1,0:T(8,128)(2,1)} %w_hbm.1) | copy-start | bytes 3145732
  3.2 1.1 %copy-start.2 = (bf16[12,49,512]{2,1,0:T(8,128)(2,1)S(1)}, bf16[12,49,512]{2,1,0:T(8,128)(2,1)}, u32[]{:S(2)}) copy-start(bf16[12,49,512]{2,1,0:T(8,128)(2,1)} %act_hbm.1) | copy-start | bytes 1806340
  4.3 0.8 %copy-start.3 = (f32[12,1024]{1,0:T(8,128)S(1)}, f32[12,1024]{1,0:T(8,128)}, u32[]{:S(2)}) copy-start(f32[12,1024]{1,0:T(8,128)} %pool_ref.1) | copy-start | bytes 147460
  5.1 0.8 %copy-start.4 = (f32[64,256]{1,0:T(8,128)S(1)}, f32[64,256]{1,0:T(8,128)}, u32[]{:S(2)}) copy-start(f32[64,256]{1,0:T(8,128)} %master_ref.1) | copy-start | bytes 196612
  6.0 0.8 %copy-start.5 = (f32[64,256]{1,0:T(8,128)S(1)}, f32[64,256]{1,0:T(8,128)}, u32[]{:S(2)}) copy-start(f32[64,256]{1,0:T(8,128)} %velocity_ref.1) | copy-start | bytes 196612
  6.8 0.7 %copy-start.6 = (f32[2,1024]{1,0:T(2,128)S(1)}, f32[2,1024]{1,0:T(2,128)}, u32[]{:S(2)}) copy-start(f32[2,1024]{1,0:T(2,128)} %bn_ref.1) | copy-start | bytes 24580
  7.5 0.7 %copy-start.7 = (f32[2,1024]{1,0:T(2,128)S(1)}, f32[2,1024]{1,0:T(2,128)}, u32[]{:S(2)}) copy-start(f32[2,1024]{1,0:T(2,128)} %bnv_ref.1) | copy-start | bytes 24580

commit v2 on v1

--- a/solution.py
+++ b/solution.py
@@ -104,12 +104,13 @@
 
 
 def kernel(
-    act_hbm, pre_hbm, pool_ref, w_hbm, master_ref, velocity_ref, bn_ref, bnv_ref,
-    ig_hbm, nm_ref, nv_ref, nw_hbm, nbn_ref, nbv_ref,
-    act, pre, w, a_s, at, conv, cg, poolg, ig, wout,
-    st_s, st_r, bn_s, bn_r, sa, ra, own, sb, rb, sc, rc, sd, rd, acc, n1s, n1r, n2s, n2r,
-    in_sem, out_sem, st_ss, st_rs, bn_ss, bn_rs, a_ss, a_rs, b_ss, b_rs, c_ss, c_rs, d_ss, d_rs,
-    n1_ss, n1_rs, n2_ss, n2_rs, z_ss, z_rs, f_ss, f_rs, g_ss, g_rs, k_ss, k_rs,
+    act_hbm, pre_hbm, pool_hbm, w_hbm, master_hbm, velocity_hbm, bn_hbm, bnv_hbm,
+    ig, nm_ref, nv_ref, nw_ref, nbn_ref, nbv_ref,
+    act, pre, pool_ref, w, master_ref, velocity_ref, bn_ref, bnv_ref,
+    a_s, at, conv, cg, poolg, base, gsum,
+    st, bn, sa, ra, own, sb, rb, sc, rc, sd, rd, acc, n1, n2,
+    in_sem, st_ss, st_rs, bn_ss, bn_rs, a_ss, a_rs, b_ss, b_rs, c_ss, c_rs, d_ss, d_rs,
+    n1_ss, n1_rs, n2_ss, n2_rs, base_ss, base_rs, gsum_ss, gsum_rs,
 ):
     images, positions, in_chan = act.shape
     out_chan = w.shape[1]
@@ -147,23 +148,120 @@
 
     loads = [
         pltpu.make_async_copy(src, dst, in_sem.at[n])
-        for n, (src, dst) in enumerate(((act_hbm, act), (w_hbm, w), (pre_hbm, pre)))
+        for n, (src, dst) in enumerate(
+            (
+                (master_hbm, master_ref),
+                (velocity_hbm, velocity_ref),
+                (w_hbm, w),
+                (act_hbm, act),
+                (pool_hbm, pool_ref),
+                (pre_hbm, pre),
+                (bn_hbm, bn_ref),
+                (bnv_hbm, bnv_ref),
+            )
+        )
     ]
     for load in loads:
         load.start()
 
+    sends = []
+
+    def block(row, p):
+        rows = pl.ds(pl.multiple_of(row * rblk, rblk), rblk)
+        return rows, pl.ds(pl.multiple_of(p * cblk, cblk), cblk)
+
+    def near_row(p):
+        h = p // 2
+        return row_of(flip(y, 1 - h), flip(x, h), k)
+
+    def far_row(p):
+        h = p // 2
+        return row_of(flip(y, h), flip(x, 1 - h), k)
+
+    diagonal = row_of(1 - y, 1 - x, k)
+    sibling = row_of(y, x, 1 - k)
+
+    class Gather:
+        def __init__(self, buf, ss, rs):
+            self.buf, self.ss, self.rs = buf, ss, rs
+
+        def copy(self, row, p, slot, to_row, to_col):
+            ref = self.buf.at[block(row, p)]
+            return pltpu.make_async_remote_copy(
+                src_ref=ref, dst_ref=ref, send_sem=self.ss.at[slot], recv_sem=self.rs.at[slot],
+                device_id=(to_row, to_col), device_id_type=MESH,
+            )
+
+        def send(self, row, p, slot, to_row, to_col):
+            copy = self.copy(row, p, slot, to_row, to_col)
+            copy.start()
+            sends.append(copy)
+
+        def along_col(self):
+            for i in range(1, n_col):
+                self.send(r, z, i, r, col_peer(i))
+
+        def own_out(self):
+            for i in range(n_col):
+                p = col_peer(i)
+                if i > 0:
+                    self.copy(r, p, i, r, p).wait_recv()
+                self.send(r, p, 4 + i, near_row(p), z)
+                self.send(r, p, 8 + i, far_row(p), z)
+                self.send(r, p, 16 + i, sibling, z)
+
+        def near_out(self):
+            for i in range(n_col):
+                p = col_peer(i)
+                got = near_row(p)
+                self.copy(got, p, 4 + i, got, z).wait_recv()
+                self.send(got, p, 12 + i, far_row(p), z)
+                self.send(got, p, 20 + i, sibling, z)
+
+        def far_out(self):
+            for i in range(n_col):
+                p = col_peer(i)
+                got = far_row(p)
+                self.copy(got, p, 8 + i, got, z).wait_recv()
+                self.send(got, p, 24 + i, sibling, z)
+            for i in range(n_col):
+                p = col_peer(i)
+                self.copy(diagonal, p, 12 + i, far_row(p), z).wait_recv()
+                self.send(diagonal, p, 28 + i, sibling, z)
+
+        def rows(self, p):
+            return (r, near_row(p), far_row(p), diagonal)
+
+        def from_sibling(self, n, i):
+            p = col_peer(i)
+            row = self.rows(p)[n] + 1 - 2 * k
+            self.copy(row, p, 16 + 4 * n + i, sibling, z).wait_recv()
+            return row, p
+
+    gather_base = Gather(base, base_ss, base_rs)
+    gather_grad = Gather(gsum, gsum_ss, gsum_rs)
+
     cg[...] = jnp.zeros_like(cg)
     a_s[...] = jnp.zeros_like(a_s)
-    poolg[...] = pool_ref[...] / positions
-    st_s[...] = jnp.zeros_like(st_s)
-    msq = jnp.sum(master_ref[...] * master_ref[...], axis=0, keepdims=True)
+    loads[0].wait()
+    loads[1].wait()
+    loads[2].wait()
+    weights_now = master_ref[...]
+    base[block(r, z)] = (
+        weights_now - w[block(r, z)].astype(jnp.float32) - momentum * velocity_ref[...]
+    ).astype(jnp.bfloat16)
+    msq = jnp.sum(weights_now * weights_now, axis=0, keepdims=True)
     m_part = functools.reduce(lambda p, q: p + q, [msq[:, c : c + 128] for c in range(0, cblk, 128)])
-
-    loads[0].wait()
+    pl.semaphore_wait(barrier, n_row + n_col - 2)
+    gather_base.along_col()
+
+    loads[3].wait()
     for im in range(images):
         a_s[PAD * im : PAD * im + positions, :] = act[im]
-    loads[1].wait()
-    loads[2].wait()
+    loads[4].wait()
+    poolg[...] = pool_ref[...] / positions
+    loads[5].wait()
+    own_st = st.at[z]
     for c in range(0, out_chan, CW):
         cols = slice(c, c + CW)
         low = jnp.dot(a_s[...], w[:, cols], preferred_element_type=jnp.float32).astype(jnp.bfloat16)
@@ -171,8 +269,8 @@
         wide = low.astype(jnp.float32)
         total = jnp.sum(wide, axis=0, keepdims=True)
         mean = total / device_count
-        st_s[0:1, cols] = total
-        st_s[1:2, cols] = jnp.sum(wide * wide, axis=0, keepdims=True)
+        own_st[0:1, cols] = total
+        own_st[1:2, cols] = jnp.sum(wide * wide, axis=0, keepdims=True)
         up_sum = jnp.zeros((1, CW), jnp.float32)
         upx_sum = jnp.zeros((1, CW), jnp.float32)
         for im in range(images):
@@ -181,21 +279,19 @@
             pooled = poolg[im : im + 1, cols]
             up_sum += pooled * jnp.sum(jnp.where(keep, 1.0, 0.0), axis=0, keepdims=True)
             upx_sum += pooled * jnp.sum(jnp.where(keep, rows - mean, 0.0), axis=0, keepdims=True)
-        st_s[2:3, cols] = up_sum
-        st_s[3:4, cols] = upx_sum
-
-    pl.semaphore_wait(barrier, n_row + n_col - 2)
-    sends = []
-    st = [
-        send(st_s, st_r.at[i - 1], st_ss.at[i - 1], st_rs.at[i - 1], r, col_peer(i))
-        for i in range(1, n_col)
+        own_st[2:3, cols] = up_sum
+        own_st[3:4, cols] = upx_sum
+
+    stats = [
+        send(st.at[z], st.at[z], st_ss.at[i - 1], st_rs.at[i - 1], r, col_peer(i)) for i in range(1, n_col)
     ]
+    gather_base.own_out()
     turned = a_s[...].T
     for q in range(n_row):
         at[q % 2, (q // 2) * rblk : (q // 2 + 1) * rblk, :] = turned[q * rblk : (q + 1) * rblk, :]
-    for copy in st:
+    for copy in stats:
         copy.wait_recv()
-    parts = [st_s[...]] + [st_r[i] for i in range(n_col - 1)]
+    parts = [st[i] for i in range(n_col)]
     mu = (parts[0][0:1] + parts[1][0:1] + parts[2][0:1] + parts[3][0:1]) / count
     square = parts[0][1:2] + parts[1][1:2] + parts[2][1:2] + parts[3][1:2]
     su = parts[0][2:3] + parts[1][2:3] + parts[2][2:3] + parts[3][2:3]
@@ -204,12 +300,15 @@
     for part in parts:
         sx += part[3:4] + (part[0:1] / device_count - mu) * part[2:3]
     sx = sx * rstd
-    bn_s[0:1, :] = sx
-    bn_s[1:2, :] = su
-    bn = [
-        send(bn_s, bn_r.at[j - 1], bn_ss.at[j - 1], bn_rs.at[j - 1], row_peer(j), z)
-        for j in range(1, n_row)
+    own_bn = bn.at[r]
+    own_bn[0:1, :] = sx
+    own_bn[1:2, :] = su
+    bns = [
+        send(bn.at[r], bn.at[r], bn_ss.at[j - 1], bn_rs.at[j - 1], row_peer(j), z) for j in range(1, n_row)
     ]
+    gather_base.near_out()
+    loads[6].wait()
+    loads[7].wait()
     scale = bn_ref[0:1, :] * rstd
     shift = scale * su / count
     slope = scale * rstd * sx / count
@@ -228,13 +327,14 @@
     for h in range(2):
         for c in range(h * half, (h + 1) * half, CW):
             grad_columns(c)
-        block = jnp.dot(at[1 - k], cg[:, h * half : (h + 1) * half], preferred_element_type=jnp.float32)
-        sa[h] = block.reshape(4, rblk, half)
+        product = jnp.dot(at[1 - k], cg[:, h * half : (h + 1) * half], preferred_element_type=jnp.float32)
+        sa[h] = product.reshape(4, rblk, half)
         core.append(send(sa.at[h], ra.at[h], a_ss.at[h], a_rs.at[h], row_of(y, x, 1 - k), z))
     for h in range(2):
-        block = jnp.dot(at[k], cg[:, h * half : (h + 1) * half], preferred_element_type=jnp.float32)
-        own[h] = block.reshape(4, rblk, half)
-
+        product = jnp.dot(at[k], cg[:, h * half : (h + 1) * half], preferred_element_type=jnp.float32)
+        own[h] = product.reshape(4, rblk, half)
+
+    gather_base.far_out()
     x_peer, y_peer = row_of(y, 1 - x, k), row_of(1 - y, x, k)
     first, second = (x_peer, y_peer), (y_peer, x_peer)
 
@@ -269,8 +369,6 @@
         sc[h] = (own[h, q] + ra[h, q] + rb[h, near].astype(jnp.float32)).astype(jnp.bfloat16)
         step_c.append(send(sc.at[h], rc.at[h], c_ss.at[h], c_rs.at[h], second[h], z))
     input_rows(images // 2, images)
-    out_copies = [pltpu.make_async_copy(ig, ig_hbm, out_sem.at[0])]
-    out_copies[0].start()
     for h in range(2):
         step_c[h].wait_recv()
         mine = y if h == 0 else x
@@ -290,117 +388,69 @@
 
     gsq = jnp.sum(grad * grad, axis=0, keepdims=True)
     g_part = functools.reduce(lambda p, q: p + q, [gsq[:, c : c + 128] for c in range(0, cblk, 128)])
-    n1s[...] = jnp.zeros_like(n1s)
-    n1s[0:1, :] = g_part
-    n1s[1:2, :] = m_part
+    own_n1 = n1.at[r]
+    own_n1[0:1, :] = g_part
+    own_n1[1:2, :] = m_part
     norm1 = [
-        send(n1s, n1r.at[j - 1], n1_ss.at[j - 1], n1_rs.at[j - 1], row_peer(j), z)
-        for j in range(1, n_row)
+        send(n1.at[r], n1.at[r], n1_ss.at[j - 1], n1_rs.at[j - 1], row_peer(j), z) for j in range(1, n_row)
     ]
-    norm = n1s[...]
-    for j in range(n_row - 1):
-        norm1[j].wait_recv()
-        norm += n1r[j]
-    n2s[...] = norm
+    gsum[block(r, z)] = grad.astype(jnp.bfloat16)
+    gather_grad.along_col()
+    for copy in norm1:
+        copy.wait_recv()
+    n2[z] = functools.reduce(lambda p, q: p + q, [n1[j] for j in range(n_row)])
     norm2 = [
-        send(n2s, n2r.at[i - 1], n2_ss.at[i - 1], n2_rs.at[i - 1], r, col_peer(i))
-        for i in range(1, n_col)
+        send(n2.at[z], n2.at[z], n2_ss.at[i - 1], n2_rs.at[i - 1], r, col_peer(i)) for i in range(1, n_col)
     ]
-    for i in range(n_col - 1):
-        norm2[i].wait_recv()
-        norm += n2r[i]
+    gather_grad.own_out()
+    for copy in norm2:
+        copy.wait_recv()
+    norm = functools.reduce(lambda p, q: p + q, [n2[i] for i in range(n_col)])
     gnorm = jnp.sqrt(jnp.sum(norm[0:1, :], axis=1, keepdims=True))
     wnorm = jnp.sqrt(jnp.sum(norm[1:2, :], axis=1, keepdims=True))
     trust = trust_coef * wnorm / (gnorm + weight_decay * wnorm)
+    rate = learn_rate * trust
+    gather_grad.near_out()
     weights_now = master_ref[...]
-    new_velocity = momentum * velocity_ref[...] + learn_rate * trust * (grad + weight_decay * weights_now)
-    new_master = weights_now - new_velocity
+    new_velocity = momentum * velocity_ref[...] + rate * (grad + weight_decay * weights_now)
     nv_ref[...] = new_velocity
-    nm_ref[...] = new_master
-
-    def block(row, p):
-        rows = pl.ds(pl.multiple_of(row * rblk, rblk), rblk)
-        return wout.at[rows, pl.ds(pl.multiple_of(p * cblk, cblk), cblk)]
-
-    def order(i):
-        return col_peer(i)
-
-    wout[pl.ds(pl.multiple_of(r * rblk, rblk), rblk), pl.ds(pl.multiple_of(z * cblk, cblk), cblk)] = (
-        new_master.astype(jnp.bfloat16)
-    )
-    zs = [
-        send(block(r, z), block(r, z), z_ss.at[i - 1], z_rs.at[i - 1], r, col_peer(i))
-        for i in range(1, n_col)
-    ]
-    sibling = row_of(y, x, 1 - k)
-
-    def near_row(p):
-        h = p // 2
-        return row_of(flip(y, 1 - h), flip(x, h), k)
-
-    def far_row(p):
-        h = p // 2
-        return row_of(flip(y, h), flip(x, 1 - h), k)
-
-    def to_sibling(row, p, slot):
-        sends.append(send(block(row, p), block(row, p), k_ss.at[slot], k_rs.at[slot], sibling, z))
-
-    near_sends, far_sends = [], []
-    for i in range(n_col):
-        p = order(i)
-        if i > 0:
-            src = block(r, p)
-            pltpu.make_async_remote_copy(
-                src_ref=src, dst_ref=src, send_sem=z_ss.at[i - 1], recv_sem=z_rs.at[i - 1],
-                device_id=(r, p), device_id_type=MESH,
-            ).wait_recv()
-        near_sends.append(send(block(r, p), block(r, p), f_ss.at[i], f_rs.at[i], near_row(p), z))
-        far_sends.append(send(block(r, p), block(r, p), g_ss.at[i], g_rs.at[i], far_row(p), z))
-        to_sibling(r, p, i)
-
-    def arrived(row, p, ss, rs, source):
-        ref = block(row, p)
-        pltpu.make_async_remote_copy(
-            src_ref=ref, dst_ref=ref, send_sem=ss, recv_sem=rs, device_id=(source, z), device_id_type=MESH
-        ).wait_recv()
-
-    for i in range(n_col):
-        p = order(i)
-        got = near_row(p)
-        arrived(got, p, f_ss.at[i], f_rs.at[i], got)
-        far_sends.append(
-            send(block(got, p), block(got, p), g_ss.at[4 + i], g_rs.at[4 + i], far_row(p), z)
-        )
-        to_sibling(got, p, 4 + i)
-    diagonal = row_of(1 - y, 1 - x, k)
-    for i in range(n_col):
-        p = order(i)
-        source = far_row(p)
-        arrived(source, p, g_ss.at[i], g_rs.at[i], source)
-        to_sibling(source, p, 8 + i)
-    for i in range(n_col):
-        p = order(i)
-        arrived(diagonal, p, g_ss.at[4 + i], g_rs.at[4 + i], far_row(p))
-        to_sibling(diagonal, p, 12 + i)
-
-    sums = bn_s[...]
-    for j in range(n_row - 1):
-        bn[j].wait_recv()
-        sums += bn_r[j]
+    nm_ref[...] = weights_now - new_velocity
+    for copy in bns:
+        copy.wait_recv()
+    sums = functools.reduce(lambda p, q: p + q, [bn[j] for j in range(n_row)])
     new_bnv = momentum * bnv_ref[...] + learn_rate * (sums * (1.0 / total_images))
     nbv_ref[...] = new_bnv
     nbn_ref[...] = bn_ref[...] - new_bnv
-
+    gather_grad.far_out()
+
+    def update(row, p):
+        at_block = block(row, p)
+        low = w[at_block].astype(jnp.float32)
+        change = base[at_block].astype(jnp.float32)
+        step = rate * (gsum[at_block].astype(jnp.float32) + weight_decay * low)
+        nw_ref[at_block] = (low + (change - step)).astype(jnp.bfloat16)
+
+    for n in range(4):
+        for i in range(n_col):
+            gather_base.from_sibling(n, i)
     for i in range(n_col):
-        p = order(i)
-        rows = (r, near_row(p), far_row(p), diagonal)
-        for n in range(4):
-            arrived(rows[n] + 1 - 2 * k, p, k_ss.at[4 * n + i], k_rs.at[4 * n + i], sibling)
-    out_copies.append(pltpu.make_async_copy(wout, nw_hbm, out_sem.at[1]))
-    out_copies[1].start()
-    for copy in st + bn + core + step_b + step_c + step_d + norm1 + norm2 + zs + near_sends + far_sends + sends:
+        for row in gather_grad.rows(col_peer(i)):
+            update(row, col_peer(i))
+    for n in range(4):
+        for i in range(n_col):
+            update(*gather_grad.from_sibling(n, i))
+    for copy in stats + bns + core + step_b + step_c + step_d + norm1 + norm2 + sends:
         copy.wait_send()
-    for copy in out_copies:
+
+
+def write_out(*refs):
+    half = len(refs) // 2
+    copies = [
+        pltpu.make_async_copy(refs[n], refs[half + n], refs[-1].at[n]) for n in range(half)
+    ]
+    for copy in copies:
+        copy.start()
+    for copy in copies:
         copy.wait()
 
 
@@ -412,37 +462,31 @@
     half = out_chan // 2
     f32, bf16 = jnp.float32, jnp.bfloat16
     vmem = pl.BlockSpec(memory_space=pltpu.VMEM)
-    hbm = pl.BlockSpec(memory_space=pl.ANY)
+    hbm = pl.BlockSpec(memory_space=pltpu.HBM)
     dma = pltpu.SemaphoreType.DMA
-    pairs = (3, 7, 2, 2, 2, 3, 7, 3, 3, 4, 8, 16)
+    pairs = (3, 7, 2, 2, 2, 3, 7, 3, 32, 32)
     flops = 6 * images * positions * in_chan * out_chan
-    return pl.pallas_call(
+    args = (activations, pre_activation, pooled_grad, weights, master, velocity, bn_params, bn_velocity)
+    shapes = tuple(
+        jax.ShapeDtypeStruct(a.shape, a.dtype)
+        for a in (activations, master, master, weights, bn_params, bn_params)
+    )
+    results = pl.pallas_call(
         kernel,
-        out_shape=(
-            jax.ShapeDtypeStruct(activations.shape, bf16),
-            jax.ShapeDtypeStruct(master.shape, f32),
-            jax.ShapeDtypeStruct(master.shape, f32),
-            jax.ShapeDtypeStruct(weights.shape, bf16),
-            jax.ShapeDtypeStruct(bn_params.shape, f32),
-            jax.ShapeDtypeStruct(bn_params.shape, f32),
-        ),
-        in_specs=[hbm, hbm, vmem, hbm, vmem, vmem, vmem, vmem],
-        out_specs=(hbm, vmem, vmem, hbm, vmem, vmem),
-        scratch_shapes=[
-            pltpu.VMEM(activations.shape, bf16),
-            pltpu.VMEM(pre_activation.shape, bf16),
-            pltpu.VMEM(weights.shape, bf16),
+        out_shape=shapes,
+        in_specs=[hbm] * len(args),
+        out_specs=(vmem,) * len(shapes),
+        scratch_shapes=[pltpu.VMEM(a.shape, a.dtype) for a in args]
+        + [
             pltpu.VMEM((rows, in_chan), bf16),
             pltpu.VMEM((2, in_chan // 2, rows), bf16),
             pltpu.VMEM((rows, out_chan), bf16),
             pltpu.VMEM((rows, out_chan), bf16),
             pltpu.VMEM(pooled_grad.shape, f32),
-            pltpu.VMEM(activations.shape, bf16),
             pltpu.VMEM(weights.shape, bf16),
-            pltpu.VMEM((4, out_chan), f32),
-            pltpu.VMEM((3, 4, out_chan), f32),
-            pltpu.VMEM((2, out_chan), f32),
-            pltpu.VMEM((7, 2, out_chan), f32),
+            pltpu.VMEM(weights.shape, bf16),
+            pltpu.VMEM((4, 4, out_chan), f32),
+            pltpu.VMEM((8, 2, out_chan), f32),
             pltpu.VMEM((2, 4, rblk, half), f32),
             pltpu.VMEM((2, 4, rblk, half), f32),
             pltpu.VMEM((2, 4, rblk, half), f32),
@@ -453,19 +497,23 @@
             pltpu.VMEM((3, rblk, cblk), bf16),
             pltpu.VMEM((3, rblk, cblk), bf16),
             pltpu.VMEM((4, rblk, cblk), f32),
-            pltpu.VMEM((8, 128), f32),
-            pltpu.VMEM((7, 8, 128), f32),
-            pltpu.VMEM((8, 128), f32),
-            pltpu.VMEM((3, 8, 128), f32),
-            dma((3,)),
-            dma((2,)),
+            pltpu.VMEM((8, 2, 128), f32),
+            pltpu.VMEM((4, 2, 128), f32),
+            dma((8,)),
         ]
         + [dma((n,)) for n in pairs for _ in range(2)],
         compiler_params=pltpu.CompilerParams(
-            collective_id=0, has_side_effects=True, vmem_limit_bytes=48 * 1024 * 1024
+            collective_id=0, has_side_effects=True, vmem_limit_bytes=32 * 1024 * 1024
         ),
         cost_estimate=pl.CostEstimate(flops=flops, bytes_accessed=8 * 1024 * 1024, transcendentals=0),
-    )(activations, pre_activation, pooled_grad, weights, master, velocity, bn_params, bn_velocity)
+    )(*args)
+    return pl.pallas_call(
+        write_out,
+        out_shape=shapes,
+        in_specs=[pl.BlockSpec(memory_space=pl.ANY)] * len(shapes),
+        out_specs=(hbm,) * len(shapes),
+        scratch_shapes=[dma((len(shapes),))],
+    )(*results)
 
 
 def pick(mesh):

time: 57.7 us -> 114 us (1.98)
  Pallas kernels: 44.7 us -> 101 us
    pallas_call x1 -> x2, Pallas kernels: 44.7 us -> 101 us  [the longest x1 58.2 us: fused(): pl.pallas_call(write_out, out_shape=shapes, in_specs=[pl.BlockSpec(memory...]
    unnamed x22 -> x28, local copies, waits for them, and re-layouts: 11.8 us -> 11.8 us
where the time goes in v2:
time: 114 us
  Pallas kernels  101 us (89%)
  local copies, waits for them, and re-layouts  11.8 us (10%)
    pallas_call x1, Pallas kernels, fused(): pl.pallas_call(write_out, out_shape=shapes, in_specs=[pl.BlockSpec(memory...  58.2 us
    pallas_call x1, Pallas kernels, fused(): pl.pallas_call(kernel, out_shape=shapes, in_specs=[hbm] * len(args), out_...  42.8 us
    unnamed x28, local copies, waits for them, and re-layouts  11.8 us

profile of v2, /device:TPU:0, one launch (start us, length us, event | category | flops | bytes accessed | tf_op | source)
XLA Modules:
  0.0 113.6 jit_solution(7092360313124515336)
XLA Ops:
  0.6 0.0 copy-start.6
  0.6 1.3 %copy-done.6 = bf16[12,49,1024]{2,1,0:T(8,128)(2,1)S(1)} copy-done((bf16[12,49,1024]{2,1,0:T(8,128)(2,1)S(1)}, bf16[12,49,1024]{2,1,0:T(8,128)(2,1)}, u32[]{:S(2)}) %copy-start.6) | copy-done | bytes 1204248
  2.0 0.0 copy-start.7
  2.0 1.2 %copy-done.7 = bf16[512,1024]{1,0:T(8,128)(2,1)S(1)} copy-done((bf16[512,1024]{1,0:T(8,128)(2,1)S(1)}, bf16[512,1024]{1,0:T(8,128)(2,1)}, u32[]{:S(2)}) %copy-start.7) | copy-done | bytes 1048600
  3.2 0.0 copy-start.8
  3.2 1.1 copy-done.8
  4.3 0.0 copy-start.9
  4.3 0.8 copy-done.9
  5.1 0.0 copy-start.10
  5.1 0.8 copy-done.10
  6.0 0.0 copy-start.11
  6.0 0.8 copy-done.11
  6.8 0.0 copy-start.12
  6.8 0.7 copy-done.12
  7.5 0.0 copy-start.13
  7.5 0.7 copy-done.13
  8.2 42.8 %shard_map.127 = (bf16[12,49,512]{2,1,0:T(8,128)(2,1)S(1)}, f32[64,256]{1,0:T(8,128)S(1)}, f32[64,256]{1,0:T(8,128)S(1)}, bf16[512,1024]{1,0:T(8,128)(2,1)S(1)},...) custom-call(bf16[12,49,512]{2,1,0:T(8,128)(2,1)S(1)} %copy-done.8, bf16[12,49,1024]{2,1,0:T(8,128)(2,1)S(1)} %copy-done.6, ...), custom_call_target="tpu_custom_call" | custom-call | flops 1849688064 | bytes 8388608 | tf_op jit(solution)/shard_map/pallas_call | solution.py:474
  51.1 0.0 copy-start
  51.1 1.0 copy-done
  52.0 0.0 copy-start.1
  52.0 0.9 copy-done.1
  52.9 0.0 copy-start.2
  52.9 0.6 copy-done.2
  53.5 0.0 copy-start.3
  53.5 0.6 copy-done.3
  54.2 0.0 copy-start.4
  54.2 0.6 copy-done.4
  54.7 0.0 copy-start.5
  54.8 0.6 copy-done.5
  55.3 58.2 %shard_map.128 = (bf16[12,49,512]{2,1,0:T(8,128)(2,1)}, f32[64,256]{1,0:T(8,128)}, f32[64,256]{1,0:T(8,128)}, bf16[512,1024]{1,0:T(8,128)(2,1)}, f32[2,1024]{1,0:T(2,128)}, /*index=5*/f32[2,1024]{1,0:T(2,128)}) custom-call(bf16[12,49,512]{2,1,0:T(8,128)(2,1)} %copy-done.1, f32[64,256]{1,0:T(8,128)} %copy-done.2, f32[64,256]{1,0:T(8,128)} %copy-done.3, ...), custom_call_target="tpu_custom_call" | custom-call | tf_op jit(solution)/shard_map/pallas_call | solution.py:510
Async XLA Ops:
  0.6 1.3 %copy-start.6 = (bf16[12,49,1024]{2,1,0:T(8,128)(2,1)S(1)}, bf16[12,49,1024]{2,1,0:T(8,128)(2,1)}, u32[]{:S(2)}) copy-start(bf16[12,49,1024]{2,1,0:T(8,128)(2,1)} %pre_hbm.1) | copy-start | bytes 3612676
  2.0 1.2 %copy-start.7 = (bf16[512,1024]{1,0:T(8,128)(2,1)S(1)}, bf16[512,1024]{1,0:T(8,128)(2,1)}, u32[]{:S(2)}) copy-start(bf16[512,1024]{1,0:T(8,128)(2,1)} %w_hbm.1) | copy-start | bytes 3145732
  3.2 1.1 copy-start.8
  4.3 0.8 copy-start.9
  5.1 0.8 copy-start.10
  6.0 0.8 copy-start.11
  6.8 0.7 copy-start.12
  7.5 0.7 copy-start.13
  51.1 1.0 copy-start
  52.0 0.9 copy-start.1
  52.9 0.6 copy-start.2
  53.5 0.6 copy-start.3
  54.2 0.6 copy-start.4
  54.7 0.6 copy-start.5

commit v3 on v2

--- a/solution.py
+++ b/solution.py
@@ -96,7 +96,7 @@
 
 MESH = pl.DeviceIdType.MESH
 PAD = 64
-CW = 256
+LIMIT = 58 * 1024 * 1024
 
 
 def flip(value, bit):
@@ -105,18 +105,18 @@
 
 def kernel(
     act_hbm, pre_hbm, pool_hbm, w_hbm, master_hbm, velocity_hbm, bn_hbm, bnv_hbm,
+    ig_hbm, nm_hbm, nv_hbm, nw_hbm, nbn_hbm, nbv_hbm,
+    act, pre, pool_ref, w, master_ref, velocity_ref, bn_ref, bnv_ref,
     ig, nm_ref, nv_ref, nw_ref, nbn_ref, nbv_ref,
-    act, pre, pool_ref, w, master_ref, velocity_ref, bn_ref, bnv_ref,
     a_s, at, conv, cg, poolg, base, gsum,
-    st, bn, sa, ra, own, sb, rb, sc, rc, sd, rd, acc, n1, n2,
-    in_sem, st_ss, st_rs, bn_ss, bn_rs, a_ss, a_rs, b_ss, b_rs, c_ss, c_rs, d_ss, d_rs,
+    st, bn, coef, sa, ra, own, sb, rb, sc, rc, sd, rd, n1, n2,
+    in_sem, out_sem, st_ss, st_rs, bn_ss, bn_rs, a_ss, a_rs, b_ss, b_rs, c_ss, c_rs, d_ss, d_rs,
     n1_ss, n1_rs, n2_ss, n2_rs, base_ss, base_rs, gsum_ss, gsum_rs,
 ):
     images, positions, in_chan = act.shape
     out_chan = w.shape[1]
     n_row, n_col = 8, 4
     rblk, cblk = in_chan // n_row, out_chan // n_col
-    half = out_chan // 2
     device_count = images * positions
     count = device_count * n_col
     total_images = images * n_row * n_col
@@ -164,7 +164,12 @@
     for load in loads:
         load.start()
 
-    sends = []
+    sends, writes = [], []
+
+    def put(src, dst):
+        copy = pltpu.make_async_copy(src, dst, out_sem.at[len(writes)])
+        copy.start()
+        writes.append(copy)
 
     def block(row, p):
         rows = pl.ds(pl.multiple_of(row * rblk, rblk), rblk)
@@ -252,46 +257,49 @@
     ).astype(jnp.bfloat16)
     msq = jnp.sum(weights_now * weights_now, axis=0, keepdims=True)
     m_part = functools.reduce(lambda p, q: p + q, [msq[:, c : c + 128] for c in range(0, cblk, 128)])
-    pl.semaphore_wait(barrier, n_row + n_col - 2)
-    gather_base.along_col()
-
     loads[3].wait()
     for im in range(images):
         a_s[PAD * im : PAD * im + positions, :] = act[im]
     loads[4].wait()
     poolg[...] = pool_ref[...] / positions
     loads[5].wait()
-    own_st = st.at[z]
-    for c in range(0, out_chan, CW):
-        cols = slice(c, c + CW)
+    stats = []
+    for part in range(n_col):
+        cols = slice(part * cblk, (part + 1) * cblk)
+        own_st = st.at[z, part]
         low = jnp.dot(a_s[...], w[:, cols], preferred_element_type=jnp.float32).astype(jnp.bfloat16)
         conv[:, cols] = low
         wide = low.astype(jnp.float32)
         total = jnp.sum(wide, axis=0, keepdims=True)
         mean = total / device_count
-        own_st[0:1, cols] = total
-        own_st[1:2, cols] = jnp.sum(wide * wide, axis=0, keepdims=True)
-        up_sum = jnp.zeros((1, CW), jnp.float32)
-        upx_sum = jnp.zeros((1, CW), jnp.float32)
+        own_st[0:1, :] = total
+        own_st[1:2, :] = jnp.sum(wide * wide, axis=0, keepdims=True)
+        up_sum = jnp.zeros((1, cblk), jnp.float32)
+        upx_sum = jnp.zeros((1, cblk), jnp.float32)
         for im in range(images):
             rows = conv[PAD * im : PAD * im + positions, cols].astype(jnp.float32)
             keep = pre[im, :, cols].astype(jnp.float32) > 0
             pooled = poolg[im : im + 1, cols]
             up_sum += pooled * jnp.sum(jnp.where(keep, 1.0, 0.0), axis=0, keepdims=True)
             upx_sum += pooled * jnp.sum(jnp.where(keep, rows - mean, 0.0), axis=0, keepdims=True)
-        own_st[2:3, cols] = up_sum
-        own_st[3:4, cols] = upx_sum
-
-    stats = [
-        send(st.at[z], st.at[z], st_ss.at[i - 1], st_rs.at[i - 1], r, col_peer(i)) for i in range(1, n_col)
-    ]
+        own_st[2:3, :] = up_sum
+        own_st[3:4, :] = upx_sum
+
+        if part == 0:
+            pl.semaphore_wait(barrier, n_row + n_col - 2)
+            gather_base.along_col()
+        for i in range(1, n_col):
+            slot = n_col * (i - 1) + part
+            stats.append(
+                send(st.at[z, part], st.at[z, part], st_ss.at[slot], st_rs.at[slot], r, col_peer(i))
+            )
     gather_base.own_out()
     turned = a_s[...].T
     for q in range(n_row):
         at[q % 2, (q // 2) * rblk : (q // 2 + 1) * rblk, :] = turned[q * rblk : (q + 1) * rblk, :]
     for copy in stats:
         copy.wait_recv()
-    parts = [st[i] for i in range(n_col)]
+    parts = [jnp.concatenate([st[i, part] for part in range(n_col)], axis=1) for i in range(n_col)]
     mu = (parts[0][0:1] + parts[1][0:1] + parts[2][0:1] + parts[3][0:1]) / count
     square = parts[0][1:2] + parts[1][1:2] + parts[2][1:2] + parts[3][1:2]
     su = parts[0][2:3] + parts[1][2:3] + parts[2][2:3] + parts[3][2:3]
@@ -310,47 +318,61 @@
     loads[6].wait()
     loads[7].wait()
     scale = bn_ref[0:1, :] * rstd
-    shift = scale * su / count
-    slope = scale * rstd * sx / count
-
-    def grad_columns(c):
-        cols = slice(c, c + CW)
+    coef[0:1, :] = scale
+    coef[1:2, :] = scale * su / count
+    coef[2:3, :] = scale * rstd * sx / count
+    coef[3:4, :] = mu
+
+    order = (3, 1, 2, 0)
+    core, step_b, step_c, step_d = [], [], [], []
+    corner = 2 * y + x
+
+    def quarter(s):
+        p = col_peer(order[s])
+        return p, p // 2
+
+    def stage_a(s):
+        p, _ = quarter(s)
+        cols = pl.ds(pl.multiple_of(p * cblk, cblk), cblk)
+        scale_c, shift_c, slope_c, mu_c = (coef[n : n + 1, cols] for n in range(4))
         for im in range(images):
             span = slice(PAD * im, PAD * im + positions)
             rows = conv[span, cols].astype(jnp.float32)
             keep = pre[im, :, cols].astype(jnp.float32) > 0
-            up = jnp.where(keep, scale[:, cols] * poolg[im : im + 1, cols], 0.0)
-            grad = up - shift[:, cols] - slope[:, cols] * (rows - mu[:, cols])
-            cg[span, cols] = grad.astype(jnp.bfloat16)
-
-    core = []
-    for h in range(2):
-        for c in range(h * half, (h + 1) * half, CW):
-            grad_columns(c)
-        product = jnp.dot(at[1 - k], cg[:, h * half : (h + 1) * half], preferred_element_type=jnp.float32)
-        sa[h] = product.reshape(4, rblk, half)
-        core.append(send(sa.at[h], ra.at[h], a_ss.at[h], a_rs.at[h], row_of(y, x, 1 - k), z))
-    for h in range(2):
-        product = jnp.dot(at[k], cg[:, h * half : (h + 1) * half], preferred_element_type=jnp.float32)
-        own[h] = product.reshape(4, rblk, half)
-
-    gather_base.far_out()
-    x_peer, y_peer = row_of(y, 1 - x, k), row_of(1 - y, x, k)
-    first, second = (x_peer, y_peer), (y_peer, x_peer)
-
-    def keep_q(h, j):
-        return 2 * j + x if h == 0 else 2 * y + j
-
-    def send_q(h, j):
-        return 2 * j + 1 - x if h == 0 else 2 * (1 - y) + j
-
-    step_b = []
-    for h in range(2):
-        core[h].wait_recv()
+            up = jnp.where(keep, scale_c * poolg[im : im + 1, cols], 0.0)
+            cg[span, cols] = (up - shift_c - slope_c * (rows - mu_c)).astype(jnp.bfloat16)
+        product = jnp.dot(at[1 - k], cg[:, cols], preferred_element_type=jnp.float32)
+        sa[s] = product.reshape(4, rblk, cblk)
+        core.append(send(sa.at[s], ra.at[s], a_ss.at[s], a_rs.at[s], sibling, z))
+        product = jnp.dot(at[k], cg[:, cols], preferred_element_type=jnp.float32)
+        own[s] = product.reshape(4, rblk, cblk)
+
+    def stage_b(s):
+        p, h = quarter(s)
+        core[s].wait_recv()
         for j in range(2):
-            q = send_q(h, j)
-            sb[h, j] = (own[h, q] + ra[h, q]).astype(jnp.bfloat16)
-        step_b.append(send(sb.at[h], rb.at[h], b_ss.at[h], b_rs.at[h], first[h], z))
+            q = (1 - h) * (2 * j + 1 - x) + h * (2 * (1 - y) + j)
+            sb[s, j] = (own[s, q] + ra[s, q]).astype(jnp.bfloat16)
+        step_b.append(send(sb.at[s], rb.at[s], b_ss.at[s], b_rs.at[s], far_row(p), z))
+
+    def stage_c(s):
+        p, h = quarter(s)
+        step_b[s].wait_recv()
+        j = (1 - h) * (1 - y) + h * (1 - x)
+        q = (1 - h) * (2 * j + x) + h * (2 * y + j)
+        sc[s] = (own[s, q] + ra[s, q] + rb[s, j].astype(jnp.float32)).astype(jnp.bfloat16)
+        step_c.append(send(sc.at[s], rc.at[s], c_ss.at[s], c_rs.at[s], near_row(p), z))
+
+    def stage_d(s):
+        p, h = quarter(s)
+        step_c[s].wait_recv()
+        j = (1 - h) * y + h * x
+        done = own[s, corner] + ra[s, corner] + rb[s, j].astype(jnp.float32) + rc[s].astype(jnp.float32)
+        if order[s] == 0:
+            return done
+        i = order[s] - 1
+        sd[i] = done.astype(jnp.bfloat16)
+        step_d.append(send(sd.at[i], rd.at[i], d_ss.at[i], d_rs.at[i], r, p))
 
     def input_rows(lo, hi):
         back = lax.dot_general(
@@ -360,29 +382,29 @@
         for im in range(lo, hi):
             ig[im] = back[PAD * (im - lo) : PAD * (im - lo) + positions, :]
 
+    stage_a(0)
+    stage_a(1)
+    stage_b(0)
+    stage_a(2)
+    stage_b(1)
+    stage_c(0)
+    stage_a(3)
+    stage_b(2)
+    stage_c(1)
+    stage_d(0)
+    stage_b(3)
     input_rows(0, images // 2)
-    step_c = []
-    for h in range(2):
-        step_b[h].wait_recv()
-        near = 1 - y if h == 0 else 1 - x
-        q = keep_q(h, near)
-        sc[h] = (own[h, q] + ra[h, q] + rb[h, near].astype(jnp.float32)).astype(jnp.bfloat16)
-        step_c.append(send(sc.at[h], rc.at[h], c_ss.at[h], c_rs.at[h], second[h], z))
+    stage_c(2)
+    stage_d(1)
+    gather_base.far_out()
+    stage_c(3)
     input_rows(images // 2, images)
-    for h in range(2):
-        step_c[h].wait_recv()
-        mine = y if h == 0 else x
-        q = 2 * y + x
-        done = own[h, q] + ra[h, q] + rb[h, mine].astype(jnp.float32) + rc[h].astype(jnp.float32)
-        acc[2 * h] = done[:, :cblk]
-        acc[2 * h + 1] = done[:, cblk:]
-    step_d = []
-    for i in range(1, n_col):
-        sd[i - 1] = acc[col_peer(i)].astype(jnp.bfloat16)
-        step_d.append(send(sd.at[i - 1], rd.at[i - 1], d_ss.at[i - 1], d_rs.at[i - 1], r, col_peer(i)))
-    grad = acc[z]
+    put(ig, ig_hbm)
+    stage_d(2)
+    grad = stage_d(3)
+    for copy in step_d:
+        copy.wait_recv()
     for i in range(n_col - 1):
-        step_d[i].wait_recv()
         grad += rd[i].astype(jnp.float32)
     grad = grad * (1.0 / total_images)
 
@@ -415,12 +437,16 @@
     new_velocity = momentum * velocity_ref[...] + rate * (grad + weight_decay * weights_now)
     nv_ref[...] = new_velocity
     nm_ref[...] = weights_now - new_velocity
+    put(nv_ref, nv_hbm)
+    put(nm_ref, nm_hbm)
     for copy in bns:
         copy.wait_recv()
     sums = functools.reduce(lambda p, q: p + q, [bn[j] for j in range(n_row)])
     new_bnv = momentum * bnv_ref[...] + learn_rate * (sums * (1.0 / total_images))
     nbv_ref[...] = new_bnv
     nbn_ref[...] = bn_ref[...] - new_bnv
+    put(nbv_ref, nbv_hbm)
+    put(nbn_ref, nbn_hbm)
     gather_grad.far_out()
 
     def update(row, p):
@@ -433,24 +459,38 @@
     for n in range(4):
         for i in range(n_col):
             gather_base.from_sibling(n, i)
-    for i in range(n_col):
-        for row in gather_grad.rows(col_peer(i)):
-            update(row, col_peer(i))
+    def put_rows(row):
+        rows = pl.ds(pl.multiple_of(row * rblk, rblk), rblk)
+        put(nw_ref.at[rows], nw_hbm.at[rows])
+
+    for n in range(4):
+        for i in range(n_col):
+            update(gather_grad.rows(col_peer(i))[n], col_peer(i))
+    for j in range(4):
+        put_rows(2 * j + k)
     for n in range(4):
         for i in range(n_col):
             update(*gather_grad.from_sibling(n, i))
+    for j in range(4):
+        put_rows(2 * j + 1 - k)
     for copy in stats + bns + core + step_b + step_c + step_d + norm1 + norm2 + sends:
         copy.wait_send()
+    for copy in writes:
+        copy.wait()
 
 
 def write_out(*refs):
-    half = len(refs) // 2
-    copies = [
-        pltpu.make_async_copy(refs[n], refs[half + n], refs[-1].at[n]) for n in range(half)
-    ]
-    for copy in copies:
+    count = len(refs) // 3
+    ins, outs, held = refs[:count], refs[count : 2 * count], refs[2 * count : 3 * count]
+    in_sem, out_sem = refs[3 * count :]
+    first = [pltpu.make_async_copy(ins[n], held[n], in_sem.at[n]) for n in range(count)]
+    second = [pltpu.make_async_copy(held[n], outs[n], out_sem.at[n]) for n in range(count)]
+    for copy in first:
         copy.start()
-    for copy in copies:
+    for n in range(count):
+        first[n].wait()
+        second[n].start()
+    for copy in second:
         copy.wait()
 
 
@@ -459,12 +499,10 @@
     out_chan = weights.shape[1]
     rows = images * PAD
     rblk, cblk = master.shape
-    half = out_chan // 2
     f32, bf16 = jnp.float32, jnp.bfloat16
-    vmem = pl.BlockSpec(memory_space=pltpu.VMEM)
     hbm = pl.BlockSpec(memory_space=pltpu.HBM)
     dma = pltpu.SemaphoreType.DMA
-    pairs = (3, 7, 2, 2, 2, 3, 7, 3, 32, 32)
+    pairs = (12, 7, 4, 4, 4, 3, 7, 3, 32, 32)
     flops = 6 * images * positions * in_chan * out_chan
     args = (activations, pre_activation, pooled_grad, weights, master, velocity, bn_params, bn_velocity)
     shapes = tuple(
@@ -475,8 +513,8 @@
         kernel,
         out_shape=shapes,
         in_specs=[hbm] * len(args),
-        out_specs=(vmem,) * len(shapes),
-        scratch_shapes=[pltpu.VMEM(a.shape, a.dtype) for a in args]
+        out_specs=(hbm,) * len(shapes),
+        scratch_shapes=[pltpu.VMEM(a.shape, a.dtype) for a in args + shapes]
         + [
             pltpu.VMEM((rows, in_chan), bf16),
             pltpu.VMEM((2, in_chan // 2, rows), bf16),
@@ -485,34 +523,36 @@
             pltpu.VMEM(pooled_grad.shape, f32),
             pltpu.VMEM(weights.shape, bf16),
             pltpu.VMEM(weights.shape, bf16),
-            pltpu.VMEM((4, 4, out_chan), f32),
+            pltpu.VMEM((4, 4, 4, cblk), f32),
             pltpu.VMEM((8, 2, out_chan), f32),
-            pltpu.VMEM((2, 4, rblk, half), f32),
-            pltpu.VMEM((2, 4, rblk, half), f32),
-            pltpu.VMEM((2, 4, rblk, half), f32),
-            pltpu.VMEM((2, 2, rblk, half), bf16),
-            pltpu.VMEM((2, 2, rblk, half), bf16),
-            pltpu.VMEM((2, rblk, half), bf16),
-            pltpu.VMEM((2, rblk, half), bf16),
+            pltpu.VMEM((4, out_chan), f32),
+            pltpu.VMEM((4, 4, rblk, cblk), f32),
+            pltpu.VMEM((4, 4, rblk, cblk), f32),
+            pltpu.VMEM((4, 4, rblk, cblk), f32),
+            pltpu.VMEM((4, 2, rblk, cblk), bf16),
+            pltpu.VMEM((4, 2, rblk, cblk), bf16),
+            pltpu.VMEM((4, rblk, cblk), bf16),
+            pltpu.VMEM((4, rblk, cblk), bf16),
             pltpu.VMEM((3, rblk, cblk), bf16),
             pltpu.VMEM((3, rblk, cblk), bf16),
-            pltpu.VMEM((4, rblk, cblk), f32),
             pltpu.VMEM((8, 2, 128), f32),
             pltpu.VMEM((4, 2, 128), f32),
             dma((8,)),
+            dma((16,)),
         ]
         + [dma((n,)) for n in pairs for _ in range(2)],
         compiler_params=pltpu.CompilerParams(
-            collective_id=0, has_side_effects=True, vmem_limit_bytes=32 * 1024 * 1024
+            collective_id=0, has_side_effects=True, vmem_limit_bytes=LIMIT
         ),
         cost_estimate=pl.CostEstimate(flops=flops, bytes_accessed=8 * 1024 * 1024, transcendentals=0),
     )(*args)
     return pl.pallas_call(
         write_out,
         out_shape=shapes,
-        in_specs=[pl.BlockSpec(memory_space=pl.ANY)] * len(shapes),
+        in_specs=[hbm] * len(shapes),
         out_specs=(hbm,) * len(shapes),
-        scratch_shapes=[dma((len(shapes),))],
+        scratch_shapes=[pltpu.VMEM(a.shape, a.dtype) for a in shapes] + [dma((len(shapes),))] * 2,
+        compiler_params=pltpu.CompilerParams(vmem_limit_bytes=LIMIT),
     )(*results)
 
 

time: 114 us -> 49.3 us (0.43)
  Pallas kernels: 101 us -> 48.5 us
  local copies, waits for them, and re-layouts: 11.8 us -> 0 us
    pallas_call x1, Pallas kernels: 58.2 us -> 2.56 us  [fused(): pl.pallas_call(write_out, out_shape=shapes, in_specs=[hbm] * len(shapes),...]
    unnamed x28 -> x0, local copies, waits for them, and re-layouts: 11.8 us -> none
    pallas_call x1, Pallas kernels: 42.8 us -> 45.9 us  [fused(): pl.pallas_call(kernel, out_shape=shapes, in_specs=[hbm] * len(args), out_...]
where the time goes in v3:
time: 49.3 us; the launch traced here: 49.1 us
  Pallas kernels  48.5 us (98%)
  between operations  0.64 us (1%)
    pallas_call x1, Pallas kernels, fused(): pl.pallas_call(kernel, out_shape=shapes, in_specs=[hbm] * len(args), out_...  45.9 us
    pallas_call x1, Pallas kernels, fused(): pl.pallas_call(write_out, out_shape=shapes, in_specs=[hbm] * len(shapes),...  2.56 us

profile of v3, /device:TPU:0, one launch (start us, length us, event | category | flops | bytes accessed | tf_op | source)
XLA Modules:
  0.0 49.1 jit_solution(13774264953166829692)
XLA Ops:
  0.6 45.9 %shard_map.127 = (bf16[12,49,512]{2,1,0:T(8,128)(2,1)}, f32[64,256]{1,0:T(8,128)}, f32[64,256]{1,0:T(8,128)}, bf16[512,1024]{1,0:T(8,128)(2,1)}, f32[2,1024]{1,0:T(2,128)}, /*index=5*/f32[2,1024]{1,0:T(2,128)}) custom-call(bf16[12,49,512]{2,1,0:T(8,128)(2,1)} %act_hbm.1, bf16[12,49,1024]{2,1,0:T(8,128)(2,1)} %pre_hbm.1, f32[12,1024]{1,0:T(8,128)} %pool_hbm.1, ...), custom_call_target="tpu_custom_call" | custom-call | flops 1849688064 | bytes 8388608 | tf_op jit(solution)/shard_map/pallas_call | solution.py:512
  46.6 2.6 %shard_map.128 = (bf16[12,49,512]{2,1,0:T(8,128)(2,1)}, f32[64,256]{1,0:T(8,128)}, f32[64,256]{1,0:T(8,128)}, bf16[512,1024]{1,0:T(8,128)(2,1)}, f32[2,1024]{1,0:T(2,128)}, /*index=5*/f32[2,1024]{1,0:T(2,128)}) custom-call(bf16[12,49,512]{2,1,0:T(8,128)(2,1)} %get-tuple-element.12.refs_0_, f32[64,256]{1,0:T(8,128)} %get-tuple-element.13.refs_1_, ...), custom_call_target="tpu_custom_call" | custom-call | tf_op jit(solution)/shard_map/pallas_call | solution.py:549

commit v4 on v3

--- a/solution.py
+++ b/solution.py
@@ -109,8 +109,8 @@
     act, pre, pool_ref, w, master_ref, velocity_ref, bn_ref, bnv_ref,
     ig, nm_ref, nv_ref, nw_ref, nbn_ref, nbv_ref,
     a_s, at, conv, cg, poolg, base, gsum,
-    st, bn, coef, sa, ra, own, sb, rb, sc, rc, sd, rd, n1, n2,
-    in_sem, out_sem, st_ss, st_rs, bn_ss, bn_rs, a_ss, a_rs, b_ss, b_rs, c_ss, c_rs, d_ss, d_rs,
+    st, coef, sa, ra, own, sb, rb, sc, rc, sd, rd, n1, n2,
+    in_sem, out_sem, st_ss, st_rs, a_ss, a_rs, b_ss, b_rs, c_ss, c_rs, d_ss, d_rs,
     n1_ss, n1_rs, n2_ss, n2_rs, base_ss, base_rs, gsum_ss, gsum_rs,
 ):
     images, positions, in_chan = act.shape
@@ -164,87 +164,93 @@
     for load in loads:
         load.start()
 
-    sends, writes = [], []
+    sends, puts = [], []
 
     def put(src, dst):
-        copy = pltpu.make_async_copy(src, dst, out_sem.at[len(writes)])
+        copy = pltpu.make_async_copy(src, dst, out_sem.at[len(puts)])
         copy.start()
-        writes.append(copy)
-
-    def block(row, p):
+        puts.append(copy)
+
+    half = 2 * cblk
+
+    def block(row, p, width):
         rows = pl.ds(pl.multiple_of(row * rblk, rblk), rblk)
-        return rows, pl.ds(pl.multiple_of(p * cblk, cblk), cblk)
-
-    def near_row(p):
-        h = p // 2
-        return row_of(flip(y, 1 - h), flip(x, h), k)
-
-    def far_row(p):
-        h = p // 2
-        return row_of(flip(y, h), flip(x, 1 - h), k)
-
-    diagonal = row_of(1 - y, 1 - x, k)
+        return rows, pl.ds(pl.multiple_of(p * width, width), width)
+
+    def plane_row(n, h, core):
+        n0, n1 = n % 2, n // 2
+        return row_of(flip(y, n0 * (1 - h) + n1 * h), flip(x, n0 * h + n1 * (1 - h)), core)
+
     sibling = row_of(y, x, 1 - k)
 
-    class Gather:
-        def __init__(self, buf, ss, rs):
-            self.buf, self.ss, self.rs = buf, ss, rs
-
-        def copy(self, row, p, slot, to_row, to_col):
-            ref = self.buf.at[block(row, p)]
-            return pltpu.make_async_remote_copy(
-                src_ref=ref, dst_ref=ref, send_sem=self.ss.at[slot], recv_sem=self.rs.at[slot],
-                device_id=(to_row, to_col), device_id_type=MESH,
-            )
-
-        def send(self, row, p, slot, to_row, to_col):
-            copy = self.copy(row, p, slot, to_row, to_col)
+    def piece(buf, ss, rs, where, slot, to_row, to_col):
+        return pltpu.make_async_remote_copy(
+            src_ref=buf.at[where], dst_ref=buf.at[where], send_sem=ss.at[slot], recv_sem=rs.at[slot],
+            device_id=(to_row, to_col), device_id_type=MESH,
+        )
+
+    def along_col(buf, ss, rs):
+        for i in range(1, n_col):
+            copy = piece(buf, ss, rs, block(r, z, cblk), i, r, col_peer(i))
             copy.start()
             sends.append(copy)
 
-        def along_col(self):
-            for i in range(1, n_col):
-                self.send(r, z, i, r, col_peer(i))
-
-        def own_out(self):
-            for i in range(n_col):
-                p = col_peer(i)
-                if i > 0:
-                    self.copy(r, p, i, r, p).wait_recv()
-                self.send(r, p, 4 + i, near_row(p), z)
-                self.send(r, p, 8 + i, far_row(p), z)
-                self.send(r, p, 16 + i, sibling, z)
-
-        def near_out(self):
-            for i in range(n_col):
-                p = col_peer(i)
-                got = near_row(p)
-                self.copy(got, p, 4 + i, got, z).wait_recv()
-                self.send(got, p, 12 + i, far_row(p), z)
-                self.send(got, p, 20 + i, sibling, z)
-
-        def far_out(self):
-            for i in range(n_col):
-                p = col_peer(i)
-                got = far_row(p)
-                self.copy(got, p, 8 + i, got, z).wait_recv()
-                self.send(got, p, 24 + i, sibling, z)
-            for i in range(n_col):
-                p = col_peer(i)
-                self.copy(diagonal, p, 12 + i, far_row(p), z).wait_recv()
-                self.send(diagonal, p, 28 + i, sibling, z)
-
-        def rows(self, p):
-            return (r, near_row(p), far_row(p), diagonal)
-
-        def from_sibling(self, n, i):
-            p = col_peer(i)
-            row = self.rows(p)[n] + 1 - 2 * k
-            self.copy(row, p, 16 + 4 * n + i, sibling, z).wait_recv()
-            return row, p
-
-    gather_base = Gather(base, base_ss, base_rs)
-    gather_grad = Gather(gsum, gsum_ss, gsum_rs)
+    def arrived_col(buf, ss, rs, i):
+        p = col_peer(i)
+        piece(buf, ss, rs, block(r, p, cblk), i, r, p).wait_recv()
+
+    def base_piece(n, slot, to_row, core=k):
+        return piece(base, base_ss, base_rs, block(plane_row(n, 0, core), 0, out_chan), slot, to_row, z)
+
+    def base_out():
+        for i in range(1, n_col):
+            arrived_col(base, base_ss, base_rs, i)
+        for n in range(1, 4):
+            copy = base_piece(0, 3 + n, plane_row(n, 0, k))
+            copy.start()
+            sends.append(copy)
+        copy = base_piece(0, 7, sibling)
+        copy.start()
+        sends.append(copy)
+
+    def base_relay():
+        for n in range(1, 4):
+            base_piece(n, 3 + n, plane_row(n, 0, k)).wait_recv()
+            copy = base_piece(n, 7 + n, sibling)
+            copy.start()
+            sends.append(copy)
+
+    def grad_piece(n, t, slot, to_row, core=k):
+        h = flip(z // 2, t)
+        return piece(gsum, gsum_ss, gsum_rs, block(plane_row(n, h, core), h, half), slot, to_row, z)
+
+    def grad_send(n, t, slot, to):
+        h = flip(z // 2, t)
+        copy = grad_piece(n, t, slot, sibling if to == 0 else plane_row(to, h, k))
+        copy.start()
+        sends.append(copy)
+
+    def grad_own_out():
+        for t in range(2):
+            for i in ((1,), (2, 3))[t]:
+                arrived_col(gsum, gsum_ss, gsum_rs, i)
+            grad_send(0, t, 4 + t, 1)
+            grad_send(0, t, 6 + t, 2)
+            grad_send(0, t, 10 + t, 0)
+
+    def grad_near_out():
+        for t in range(2):
+            grad_piece(1, t, 4 + t, sibling).wait_recv()
+            grad_send(1, t, 8 + t, 2)
+            grad_send(1, t, 12 + t, 0)
+
+    def grad_far_out():
+        for t in range(2):
+            grad_piece(2, t, 6 + t, sibling).wait_recv()
+            grad_send(2, t, 14 + t, 0)
+        for t in range(2):
+            grad_piece(3, t, 8 + t, sibling).wait_recv()
+            grad_send(3, t, 16 + t, 0)
 
     cg[...] = jnp.zeros_like(cg)
     a_s[...] = jnp.zeros_like(a_s)
@@ -252,20 +258,23 @@
     loads[1].wait()
     loads[2].wait()
     weights_now = master_ref[...]
-    base[block(r, z)] = (
-        weights_now - w[block(r, z)].astype(jnp.float32) - momentum * velocity_ref[...]
+    base[block(r, z, cblk)] = (
+        weights_now - w[block(r, z, cblk)].astype(jnp.float32) - momentum * velocity_ref[...]
     ).astype(jnp.bfloat16)
     msq = jnp.sum(weights_now * weights_now, axis=0, keepdims=True)
     m_part = functools.reduce(lambda p, q: p + q, [msq[:, c : c + 128] for c in range(0, cblk, 128)])
+    pl.semaphore_wait(barrier, n_row + n_col - 2)
+    along_col(base, base_ss, base_rs)
     loads[3].wait()
     for im in range(images):
         a_s[PAD * im : PAD * im + positions, :] = act[im]
     loads[4].wait()
     poolg[...] = pool_ref[...] / positions
     loads[5].wait()
-    stats = []
-    for part in range(n_col):
-        cols = slice(part * cblk, (part + 1) * cblk)
+
+    @pl.loop(0, n_col)
+    def conv_columns(part):
+        cols = pl.ds(pl.multiple_of(part * cblk, cblk), cblk)
         own_st = st.at[z, part]
         low = jnp.dot(a_s[...], w[:, cols], preferred_element_type=jnp.float32).astype(jnp.bfloat16)
         conv[:, cols] = low
@@ -285,15 +294,11 @@
         own_st[2:3, :] = up_sum
         own_st[3:4, :] = upx_sum
 
-        if part == 0:
-            pl.semaphore_wait(barrier, n_row + n_col - 2)
-            gather_base.along_col()
-        for i in range(1, n_col):
-            slot = n_col * (i - 1) + part
-            stats.append(
-                send(st.at[z, part], st.at[z, part], st_ss.at[slot], st_rs.at[slot], r, col_peer(i))
-            )
-    gather_base.own_out()
+
+    stats = [
+        send(st.at[z], st.at[z], st_ss.at[i - 1], st_rs.at[i - 1], r, col_peer(i)) for i in range(1, n_col)
+    ]
+    base_out()
     turned = a_s[...].T
     for q in range(n_row):
         at[q % 2, (q // 2) * rblk : (q // 2 + 1) * rblk, :] = turned[q * rblk : (q + 1) * rblk, :]
@@ -308,13 +313,9 @@
     for part in parts:
         sx += part[3:4] + (part[0:1] / device_count - mu) * part[2:3]
     sx = sx * rstd
-    own_bn = bn.at[r]
-    own_bn[0:1, :] = sx
-    own_bn[1:2, :] = su
-    bns = [
-        send(bn.at[r], bn.at[r], bn_ss.at[j - 1], bn_rs.at[j - 1], row_peer(j), z) for j in range(1, n_row)
-    ]
-    gather_base.near_out()
+    own_n1 = n1.at[r]
+    own_n1[0:1, :out_chan] = sx
+    own_n1[1:2, :out_chan] = su
     loads[6].wait()
     loads[7].wait()
     scale = bn_ref[0:1, :] * rstd
@@ -323,16 +324,34 @@
     coef[2:3, :] = scale * rstd * sx / count
     coef[3:4, :] = mu
 
-    order = (3, 1, 2, 0)
-    core, step_b, step_c, step_d = [], [], [], []
     corner = 2 * y + x
 
     def quarter(s):
-        p = col_peer(order[s])
-        return p, p // 2
+        i = 2 * (1 - s % 2) + 1 - s // 2
+        p = 2 * flip(z // 2, 1 - s % 2) + flip(lax.rem(z, 2), 1 - s // 2)
+        return i, p, p // 2
+
+    def remote(src, dst, ss, rs, row, col):
+        return pltpu.make_async_remote_copy(
+            src_ref=src, dst_ref=dst, send_sem=ss, recv_sem=rs,
+            device_id=(row, col), device_id_type=MESH,
+        )
+
+    def copy_a(s):
+        return remote(sa.at[s], ra.at[s], a_ss.at[s], a_rs.at[s], sibling, z)
+
+    def copy_b(s):
+        return remote(sb.at[s], rb.at[s], b_ss.at[s], b_rs.at[s], plane_row(2, quarter(s)[2], k), z)
+
+    def copy_c(s):
+        return remote(sc.at[s], rc.at[s], c_ss.at[s], c_rs.at[s], plane_row(1, quarter(s)[2], k), z)
+
+    def copy_d(s):
+        i, p, _ = quarter(s)
+        return remote(sd.at[s], rd.at[s], d_ss.at[s], d_rs.at[s], r, p)
 
     def stage_a(s):
-        p, _ = quarter(s)
+        _, p, _ = quarter(s)
         cols = pl.ds(pl.multiple_of(p * cblk, cblk), cblk)
         scale_c, shift_c, slope_c, mu_c = (coef[n : n + 1, cols] for n in range(4))
         for im in range(images):
@@ -343,36 +362,35 @@
             cg[span, cols] = (up - shift_c - slope_c * (rows - mu_c)).astype(jnp.bfloat16)
         product = jnp.dot(at[1 - k], cg[:, cols], preferred_element_type=jnp.float32)
         sa[s] = product.reshape(4, rblk, cblk)
-        core.append(send(sa.at[s], ra.at[s], a_ss.at[s], a_rs.at[s], sibling, z))
+        copy_a(s).start()
         product = jnp.dot(at[k], cg[:, cols], preferred_element_type=jnp.float32)
         own[s] = product.reshape(4, rblk, cblk)
 
     def stage_b(s):
-        p, h = quarter(s)
-        core[s].wait_recv()
+        _, _, h = quarter(s)
+        copy_a(s).wait_recv()
         for j in range(2):
             q = (1 - h) * (2 * j + 1 - x) + h * (2 * (1 - y) + j)
             sb[s, j] = (own[s, q] + ra[s, q]).astype(jnp.bfloat16)
-        step_b.append(send(sb.at[s], rb.at[s], b_ss.at[s], b_rs.at[s], far_row(p), z))
+        copy_b(s).start()
 
     def stage_c(s):
-        p, h = quarter(s)
-        step_b[s].wait_recv()
+        _, _, h = quarter(s)
+        copy_b(s).wait_recv()
         j = (1 - h) * (1 - y) + h * (1 - x)
         q = (1 - h) * (2 * j + x) + h * (2 * y + j)
         sc[s] = (own[s, q] + ra[s, q] + rb[s, j].astype(jnp.float32)).astype(jnp.bfloat16)
-        step_c.append(send(sc.at[s], rc.at[s], c_ss.at[s], c_rs.at[s], near_row(p), z))
+        copy_c(s).start()
 
     def stage_d(s):
-        p, h = quarter(s)
-        step_c[s].wait_recv()
+        _, _, h = quarter(s)
+        copy_c(s).wait_recv()
         j = (1 - h) * y + h * x
         done = own[s, corner] + ra[s, corner] + rb[s, j].astype(jnp.float32) + rc[s].astype(jnp.float32)
-        if order[s] == 0:
+        if isinstance(s, int) and s == 3:
             return done
-        i = order[s] - 1
-        sd[i] = done.astype(jnp.bfloat16)
-        step_d.append(send(sd.at[i], rd.at[i], d_ss.at[i], d_rs.at[i], r, p))
+        sd[s] = done.astype(jnp.bfloat16)
+        copy_d(s).start()
 
     def input_rows(lo, hi):
         back = lax.dot_general(
@@ -382,49 +400,45 @@
         for im in range(lo, hi):
             ig[im] = back[PAD * (im - lo) : PAD * (im - lo) + positions, :]
 
-    stage_a(0)
-    stage_a(1)
-    stage_b(0)
-    stage_a(2)
-    stage_b(1)
-    stage_c(0)
-    stage_a(3)
-    stage_b(2)
-    stage_c(1)
+    @pl.loop(0, 4)
+    def reduce_quarters(s):
+        stage_a(s)
+        pl.when(s >= 1)(lambda: stage_b(s - 1))
+        pl.when(s >= 2)(lambda: stage_c(s - 2))
+
+    stage_b(3)
     stage_d(0)
-    stage_b(3)
     input_rows(0, images // 2)
     stage_c(2)
     stage_d(1)
-    gather_base.far_out()
+    base_relay()
     stage_c(3)
     input_rows(images // 2, images)
     put(ig, ig_hbm)
     stage_d(2)
     grad = stage_d(3)
-    for copy in step_d:
-        copy.wait_recv()
     for i in range(n_col - 1):
+        copy_d(i).wait_recv()
         grad += rd[i].astype(jnp.float32)
     grad = grad * (1.0 / total_images)
 
     gsq = jnp.sum(grad * grad, axis=0, keepdims=True)
     g_part = functools.reduce(lambda p, q: p + q, [gsq[:, c : c + 128] for c in range(0, cblk, 128)])
-    own_n1 = n1.at[r]
-    own_n1[0:1, :] = g_part
-    own_n1[1:2, :] = m_part
+    own_n1[0:1, out_chan:] = g_part
+    own_n1[1:2, out_chan:] = m_part
     norm1 = [
         send(n1.at[r], n1.at[r], n1_ss.at[j - 1], n1_rs.at[j - 1], row_peer(j), z) for j in range(1, n_row)
     ]
-    gsum[block(r, z)] = grad.astype(jnp.bfloat16)
-    gather_grad.along_col()
+    gsum[block(r, z, cblk)] = grad.astype(jnp.bfloat16)
+    along_col(gsum, gsum_ss, gsum_rs)
     for copy in norm1:
         copy.wait_recv()
-    n2[z] = functools.reduce(lambda p, q: p + q, [n1[j] for j in range(n_row)])
+    all_sums = functools.reduce(lambda p, q: p + q, [n1[j] for j in range(n_row)])
+    n2[z] = all_sums[:, out_chan:]
     norm2 = [
         send(n2.at[z], n2.at[z], n2_ss.at[i - 1], n2_rs.at[i - 1], r, col_peer(i)) for i in range(1, n_col)
     ]
-    gather_grad.own_out()
+    grad_own_out()
     for copy in norm2:
         copy.wait_recv()
     norm = functools.reduce(lambda p, q: p + q, [n2[i] for i in range(n_col)])
@@ -432,50 +446,51 @@
     wnorm = jnp.sqrt(jnp.sum(norm[1:2, :], axis=1, keepdims=True))
     trust = trust_coef * wnorm / (gnorm + weight_decay * wnorm)
     rate = learn_rate * trust
-    gather_grad.near_out()
+    grad_near_out()
     weights_now = master_ref[...]
     new_velocity = momentum * velocity_ref[...] + rate * (grad + weight_decay * weights_now)
     nv_ref[...] = new_velocity
     nm_ref[...] = weights_now - new_velocity
     put(nv_ref, nv_hbm)
     put(nm_ref, nm_hbm)
-    for copy in bns:
-        copy.wait_recv()
-    sums = functools.reduce(lambda p, q: p + q, [bn[j] for j in range(n_row)])
+    sums = all_sums[:, :out_chan]
     new_bnv = momentum * bnv_ref[...] + learn_rate * (sums * (1.0 / total_images))
     nbv_ref[...] = new_bnv
     nbn_ref[...] = bn_ref[...] - new_bnv
     put(nbv_ref, nbv_hbm)
     put(nbn_ref, nbn_hbm)
-    gather_grad.far_out()
-
-    def update(row, p):
-        at_block = block(row, p)
+    grad_far_out()
+
+    def update(at_block):
         low = w[at_block].astype(jnp.float32)
         change = base[at_block].astype(jnp.float32)
         step = rate * (gsum[at_block].astype(jnp.float32) + weight_decay * low)
         nw_ref[at_block] = (low + (change - step)).astype(jnp.bfloat16)
 
+    @pl.loop(0, 8)
+    def update_own(e):
+        update(block(2 * (e // 2) + k, e % 2, half))
+
     for n in range(4):
-        for i in range(n_col):
-            gather_base.from_sibling(n, i)
-    def put_rows(row):
-        rows = pl.ds(pl.multiple_of(row * rblk, rblk), rblk)
-        put(nw_ref.at[rows], nw_hbm.at[rows])
-
-    for n in range(4):
-        for i in range(n_col):
-            update(gather_grad.rows(col_peer(i))[n], col_peer(i))
-    for j in range(4):
-        put_rows(2 * j + k)
-    for n in range(4):
-        for i in range(n_col):
-            update(*gather_grad.from_sibling(n, i))
-    for j in range(4):
-        put_rows(2 * j + 1 - k)
-    for copy in stats + bns + core + step_b + step_c + step_d + norm1 + norm2 + sends:
+        base_piece(n, 7 + n, sibling, 1 - k).wait_recv()
+
+    @pl.loop(0, 8)
+    def update_other(e):
+        n, t = e // 2, e % 2
+        grad_piece(n, t, 10 + e, sibling, 1 - k).wait_recv()
+        h = flip(z // 2, t)
+        update(block(plane_row(n, h, 1 - k), h, half))
+
+    put(nw_ref, nw_hbm)
+    for copy in stats + norm1 + norm2 + sends:
         copy.wait_send()
-    for copy in writes:
+    for s in range(4):
+        copy_a(s).wait_send()
+        copy_b(s).wait_send()
+        copy_c(s).wait_send()
+        if s < 3:
+            copy_d(s).wait_send()
+    for copy in puts:
         copy.wait()
 
 
@@ -502,7 +517,7 @@
     f32, bf16 = jnp.float32, jnp.bfloat16
     hbm = pl.BlockSpec(memory_space=pltpu.HBM)
     dma = pltpu.SemaphoreType.DMA
-    pairs = (12, 7, 4, 4, 4, 3, 7, 3, 32, 32)
+    pairs = (3, 4, 4, 4, 3, 7, 3, 11, 18)
     flops = 6 * images * positions * in_chan * out_chan
     args = (activations, pre_activation, pooled_grad, weights, master, velocity, bn_params, bn_velocity)
     shapes = tuple(
@@ -524,7 +539,6 @@
             pltpu.VMEM(weights.shape, bf16),
             pltpu.VMEM(weights.shape, bf16),
             pltpu.VMEM((4, 4, 4, cblk), f32),
-            pltpu.VMEM((8, 2, out_chan), f32),
             pltpu.VMEM((4, out_chan), f32),
             pltpu.VMEM((4, 4, rblk, cblk), f32),
             pltpu.VMEM((4, 4, rblk, cblk), f32),
@@ -535,7 +549,7 @@
             pltpu.VMEM((4, rblk, cblk), bf16),
             pltpu.VMEM((3, rblk, cblk), bf16),
             pltpu.VMEM((3, rblk, cblk), bf16),
-            pltpu.VMEM((8, 2, 128), f32),
+            pltpu.VMEM((8, 2, out_chan + 128), f32),
             pltpu.VMEM((4, 2, 128), f32),
             dma((8,)),
             dma((16,)),

time: 49.3 us -> 46.8 us (0.949)
  Pallas kernels: 48.5 us -> 46 us
    pallas_call x1, Pallas kernels: 45.9 us -> 43.5 us  [fused(): pl.pallas_call(kernel, out_shape=shapes, in_specs=[hbm] * len(args), out_...]
where the time goes in v4:
time: 46.8 us; the launch traced here: 46.7 us
  Pallas kernels  46 us (98%)
  between operations  0.64 us (1%)
    pallas_call x1, Pallas kernels, fused(): pl.pallas_call(kernel, out_shape=shapes, in_specs=[hbm] * len(args), out_...  43.5 us
    pallas_call x1, Pallas kernels, fused(): pl.pallas_call(write_out, out_shape=shapes, in_specs=[hbm] * len(shapes),...  2.56 us

profile of v4, /device:TPU:0, one launch (start us, length us, event | category | flops | bytes accessed | tf_op | source)
XLA Modules:
  0.0 46.7 jit_solution(671851323131805069)
XLA Ops:
  0.6 43.5 %shard_map.127 = (bf16[12,49,512]{2,1,0:T(8,128)(2,1)}, f32[64,256]{1,0:T(8,128)}, f32[64,256]{1,0:T(8,128)}, bf16[512,1024]{1,0:T(8,128)(2,1)}, f32[2,1024]{1,0:T(2,128)}, /*index=5*/f32[2,1024]{1,0:T(2,128)}) custom-call(bf16[12,49,512]{2,1,0:T(8,128)(2,1)} %act_hbm.1, bf16[12,49,1024]{2,1,0:T(8,128)(2,1)} %pre_hbm.1, f32[12,1024]{1,0:T(8,128)} %pool_hbm.1, ...), custom_call_target="tpu_custom_call" | custom-call | flops 1849688064 | bytes 8388608 | tf_op jit(solution)/shard_map/pallas_call | solution.py:527
  44.1 2.6 %shard_map.128 = (bf16[12,49,512]{2,1,0:T(8,128)(2,1)}, f32[64,256]{1,0:T(8,128)}, f32[64,256]{1,0:T(8,128)}, bf16[512,1024]{1,0:T(8,128)(2,1)}, f32[2,1024]{1,0:T(2,128)}, /*index=5*/f32[2,1024]{1,0:T(2,128)}) custom-call(bf16[12,49,512]{2,1,0:T(8,128)(2,1)} %get-tuple-element.12.refs_0_, f32[64,256]{1,0:T(8,128)} %get-tuple-element.13.refs_1_, ...), custom_call_target="tpu_custom_call" | custom-call | tf_op jit(solution)/shard_map/pallas_call | solution.py:563

commit v5 on v4

--- a/solution.py
+++ b/solution.py
@@ -230,13 +230,12 @@
         copy.start()
         sends.append(copy)
 
-    def grad_own_out():
-        for t in range(2):
-            for i in ((1,), (2, 3))[t]:
-                arrived_col(gsum, gsum_ss, gsum_rs, i)
-            grad_send(0, t, 4 + t, 1)
-            grad_send(0, t, 6 + t, 2)
-            grad_send(0, t, 10 + t, 0)
+    def grad_own_out(t):
+        for i in ((1,), (2, 3))[t]:
+            arrived_col(gsum, gsum_ss, gsum_rs, i)
+        grad_send(0, t, 4 + t, 1)
+        grad_send(0, t, 6 + t, 2)
+        grad_send(0, t, 10 + t, 0)
 
     def grad_near_out():
         for t in range(2):
@@ -272,7 +271,6 @@
     poolg[...] = pool_ref[...] / positions
     loads[5].wait()
 
-    @pl.loop(0, n_col)
     def conv_columns(part):
         cols = pl.ds(pl.multiple_of(part * cblk, cblk), cblk)
         own_st = st.at[z, part]
@@ -294,11 +292,12 @@
         own_st[2:3, :] = up_sum
         own_st[3:4, :] = upx_sum
 
-
+    pl.loop(0, 2)(conv_columns)
+    base_out()
+    pl.loop(2, n_col)(conv_columns)
     stats = [
         send(st.at[z], st.at[z], st_ss.at[i - 1], st_rs.at[i - 1], r, col_peer(i)) for i in range(1, n_col)
     ]
-    base_out()
     turned = a_s[...].T
     for q in range(n_row):
         at[q % 2, (q // 2) * rblk : (q // 2 + 1) * rblk, :] = turned[q * rblk : (q + 1) * rblk, :]
@@ -360,18 +359,18 @@
             keep = pre[im, :, cols].astype(jnp.float32) > 0
             up = jnp.where(keep, scale_c * poolg[im : im + 1, cols], 0.0)
             cg[span, cols] = (up - shift_c - slope_c * (rows - mu_c)).astype(jnp.bfloat16)
-        product = jnp.dot(at[1 - k], cg[:, cols], preferred_element_type=jnp.float32)
-        sa[s] = product.reshape(4, rblk, cblk)
+        both = at[...].reshape(in_chan, images * PAD)
+        product = jnp.dot(both, cg[:, cols], preferred_element_type=jnp.float32)
+        own[s] = product.reshape(2, 4, rblk, cblk)
+        sa[s] = own[s, 1 - k].astype(jnp.bfloat16)
         copy_a(s).start()
-        product = jnp.dot(at[k], cg[:, cols], preferred_element_type=jnp.float32)
-        own[s] = product.reshape(4, rblk, cblk)
 
     def stage_b(s):
         _, _, h = quarter(s)
         copy_a(s).wait_recv()
         for j in range(2):
             q = (1 - h) * (2 * j + 1 - x) + h * (2 * (1 - y) + j)
-            sb[s, j] = (own[s, q] + ra[s, q]).astype(jnp.bfloat16)
+            sb[s, j] = (own[s, k, q] + ra[s, q].astype(jnp.float32)).astype(jnp.bfloat16)
         copy_b(s).start()
 
     def stage_c(s):
@@ -379,14 +378,14 @@
         copy_b(s).wait_recv()
         j = (1 - h) * (1 - y) + h * (1 - x)
         q = (1 - h) * (2 * j + x) + h * (2 * y + j)
-        sc[s] = (own[s, q] + ra[s, q] + rb[s, j].astype(jnp.float32)).astype(jnp.bfloat16)
+        sc[s] = (own[s, k, q] + ra[s, q].astype(jnp.float32) + rb[s, j].astype(jnp.float32)).astype(jnp.bfloat16)
         copy_c(s).start()
 
     def stage_d(s):
         _, _, h = quarter(s)
         copy_c(s).wait_recv()
         j = (1 - h) * y + h * x
-        done = own[s, corner] + ra[s, corner] + rb[s, j].astype(jnp.float32) + rc[s].astype(jnp.float32)
+        done = own[s, k, corner] + ra[s, corner].astype(jnp.float32) + rb[s, j].astype(jnp.float32) + rc[s].astype(jnp.float32)
         if isinstance(s, int) and s == 3:
             return done
         sd[s] = done.astype(jnp.bfloat16)
@@ -408,14 +407,12 @@
 
     stage_b(3)
     stage_d(0)
-    input_rows(0, images // 2)
     stage_c(2)
     stage_d(1)
+    stage_c(3)
     base_relay()
-    stage_c(3)
-    input_rows(images // 2, images)
-    put(ig, ig_hbm)
     stage_d(2)
+    input_rows(0, images // 2)
     grad = stage_d(3)
     for i in range(n_col - 1):
         copy_d(i).wait_recv()
@@ -431,6 +428,9 @@
     ]
     gsum[block(r, z, cblk)] = grad.astype(jnp.bfloat16)
     along_col(gsum, gsum_ss, gsum_rs)
+    input_rows(images // 2, images)
+    put(ig, ig_hbm)
+    grad_own_out(0)
     for copy in norm1:
         copy.wait_recv()
     all_sums = functools.reduce(lambda p, q: p + q, [n1[j] for j in range(n_row)])
@@ -438,7 +438,14 @@
     norm2 = [
         send(n2.at[z], n2.at[z], n2_ss.at[i - 1], n2_rs.at[i - 1], r, col_peer(i)) for i in range(1, n_col)
     ]
-    grad_own_out()
+    grad_own_out(1)
+    sums = all_sums[:, :out_chan]
+    new_bnv = momentum * bnv_ref[...] + learn_rate * (sums * (1.0 / total_images))
+    nbv_ref[...] = new_bnv
+    nbn_ref[...] = bn_ref[...] - new_bnv
+    put(nbv_ref, nbv_hbm)
+    put(nbn_ref, nbn_hbm)
+    grad_near_out()
     for copy in norm2:
         copy.wait_recv()
     norm = functools.reduce(lambda p, q: p + q, [n2[i] for i in range(n_col)])
@@ -446,19 +453,12 @@
     wnorm = jnp.sqrt(jnp.sum(norm[1:2, :], axis=1, keepdims=True))
     trust = trust_coef * wnorm / (gnorm + weight_decay * wnorm)
     rate = learn_rate * trust
-    grad_near_out()
     weights_now = master_ref[...]
     new_velocity = momentum * velocity_ref[...] + rate * (grad + weight_decay * weights_now)
     nv_ref[...] = new_velocity
     nm_ref[...] = weights_now - new_velocity
     put(nv_ref, nv_hbm)
     put(nm_ref, nm_hbm)
-    sums = all_sums[:, :out_chan]
-    new_bnv = momentum * bnv_ref[...] + learn_rate * (sums * (1.0 / total_images))
-    nbv_ref[...] = new_bnv
-    nbn_ref[...] = bn_ref[...] - new_bnv
-    put(nbv_ref, nbv_hbm)
-    put(nbn_ref, nbn_hbm)
     grad_far_out()
 
     def update(at_block):
@@ -498,13 +498,21 @@
     count = len(refs) // 3
     ins, outs, held = refs[:count], refs[count : 2 * count], refs[2 * count : 3 * count]
     in_sem, out_sem = refs[3 * count :]
-    first = [pltpu.make_async_copy(ins[n], held[n], in_sem.at[n]) for n in range(count)]
-    second = [pltpu.make_async_copy(held[n], outs[n], out_sem.at[n]) for n in range(count)]
+    moves = []
+    for n in range(count):
+        size = ins[n].shape[0]
+        pieces = 4 if size % 64 == 0 and ins[n].dtype == jnp.bfloat16 else 1
+        step = size // pieces
+        for part in range(pieces):
+            rows = pl.ds(part * step, step)
+            moves.append((ins[n].at[rows], held[n].at[rows], outs[n].at[rows]))
+    first = [pltpu.make_async_copy(a, b, in_sem.at[m]) for m, (a, b, _) in enumerate(moves)]
+    second = [pltpu.make_async_copy(b, c, out_sem.at[m]) for m, (_, b, c) in enumerate(moves)]
     for copy in first:
         copy.start()
-    for n in range(count):
-        first[n].wait()
-        second[n].start()
+    for m in range(len(moves)):
+        first[m].wait()
+        second[m].start()
     for copy in second:
         copy.wait()
 
@@ -540,9 +548,9 @@
             pltpu.VMEM(weights.shape, bf16),
             pltpu.VMEM((4, 4, 4, cblk), f32),
             pltpu.VMEM((4, out_chan), f32),
-            pltpu.VMEM((4, 4, rblk, cblk), f32),
-            pltpu.VMEM((4, 4, rblk, cblk), f32),
-            pltpu.VMEM((4, 4, rblk, cblk), f32),
+            pltpu.VMEM((4, 4, rblk, cblk), bf16),
+            pltpu.VMEM((4, 4, rblk, cblk), bf16),
+            pltpu.VMEM((4, 2, 4, rblk, cblk), f32),
             pltpu.VMEM((4, 2, rblk, cblk), bf16),
             pltpu.VMEM((4, 2, rblk, cblk), bf16),
             pltpu.VMEM((4, rblk, cblk), bf16),
@@ -565,7 +573,7 @@
         out_shape=shapes,
         in_specs=[hbm] * len(shapes),
         out_specs=(hbm,) * len(shapes),
-        scratch_shapes=[pltpu.VMEM(a.shape, a.dtype) for a in shapes] + [dma((len(shapes),))] * 2,
+        scratch_shapes=[pltpu.VMEM(a.shape, a.dtype) for a in shapes] + [dma((16,))] * 2,
         compiler_params=pltpu.CompilerParams(vmem_limit_bytes=LIMIT),
     )(*results)
 

time: 46.8 us -> 48.9 us (1.045)
  Pallas kernels: 46 us -> 48.1 us
    pallas_call x1, Pallas kernels: 43.5 us -> 45.5 us  [fused(): pl.pallas_call(kernel, out_shape=shapes, in_specs=[hbm] * len(args), out_...]
where the time goes in v5:
time: 48.9 us; the launch traced here: 48.7 us
  Pallas kernels  48.1 us (98%)
  between operations  0.64 us (1%)
    pallas_call x1, Pallas kernels, fused(): pl.pallas_call(kernel, out_shape=shapes, in_specs=[hbm] * len(args), out_...  45.5 us
    pallas_call x1, Pallas kernels, fused(): pl.pallas_call(write_out, out_shape=shapes, in_specs=[hbm] * len(shapes),...  2.62 us

profile of v5, /device:TPU:0, one launch (start us, length us, event | category | flops | bytes accessed | tf_op | source)
XLA Modules:
  0.0 48.7 jit_solution(10752625521568947741)
XLA Ops:
  0.6 45.5 %shard_map.127 = (bf16[12,49,512]{2,1,0:T(8,128)(2,1)}, f32[64,256]{1,0:T(8,128)}, f32[64,256]{1,0:T(8,128)}, bf16[512,1024]{1,0:T(8,128)(2,1)}, f32[2,1024]{1,0:T(2,128)}, /*index=5*/f32[2,1024]{1,0:T(2,128)}) custom-call(bf16[12,49,512]{2,1,0:T(8,128)(2,1)} %act_hbm.1, bf16[12,49,1024]{2,1,0:T(8,128)(2,1)} %pre_hbm.1, f32[12,1024]{1,0:T(8,128)} %pool_hbm.1, ...), custom_call_target="tpu_custom_call" | custom-call | flops 1849688064 | bytes 8388608 | tf_op jit(solution)/shard_map/pallas_call | solution.py:535
  46.1 2.6 %shard_map.128 = (bf16[12,49,512]{2,1,0:T(8,128)(2,1)}, f32[64,256]{1,0:T(8,128)}, f32[64,256]{1,0:T(8,128)}, bf16[512,1024]{1,0:T(8,128)(2,1)}, f32[2,1024]{1,0:T(2,128)}, /*index=5*/f32[2,1024]{1,0:T(2,128)}) custom-call(bf16[12,49,512]{2,1,0:T(8,128)(2,1)} %get-tuple-element.12.refs_0_, f32[64,256]{1,0:T(8,128)} %get-tuple-element.13.refs_1_, ...), custom_call_target="tpu_custom_call" | custom-call | tf_op jit(solution)/shard_map/pallas_call | solution.py:571

commit v6 on v5

--- a/solution.py
+++ b/solution.py
@@ -292,15 +292,14 @@
         own_st[2:3, :] = up_sum
         own_st[3:4, :] = upx_sum
 
-    pl.loop(0, 2)(conv_columns)
-    base_out()
-    pl.loop(2, n_col)(conv_columns)
+    pl.loop(0, n_col)(conv_columns)
     stats = [
         send(st.at[z], st.at[z], st_ss.at[i - 1], st_rs.at[i - 1], r, col_peer(i)) for i in range(1, n_col)
     ]
     turned = a_s[...].T
     for q in range(n_row):
         at[q % 2, (q // 2) * rblk : (q // 2 + 1) * rblk, :] = turned[q * rblk : (q + 1) * rblk, :]
+    base_out()
     for copy in stats:
         copy.wait_recv()
     parts = [jnp.concatenate([st[i, part] for part in range(n_col)], axis=1) for i in range(n_col)]
@@ -407,12 +406,14 @@
 
     stage_b(3)
     stage_d(0)
+    input_rows(0, images // 2)
     stage_c(2)
     stage_d(1)
+    base_relay()
     stage_c(3)
-    base_relay()
+    input_rows(images // 2, images)
+    put(ig, ig_hbm)
     stage_d(2)
-    input_rows(0, images // 2)
     grad = stage_d(3)
     for i in range(n_col - 1):
         copy_d(i).wait_recv()
@@ -428,8 +429,6 @@
     ]
     gsum[block(r, z, cblk)] = grad.astype(jnp.bfloat16)
     along_col(gsum, gsum_ss, gsum_rs)
-    input_rows(images // 2, images)
-    put(ig, ig_hbm)
     grad_own_out(0)
     for copy in norm1:
         copy.wait_recv()
@@ -498,21 +497,13 @@
     count = len(refs) // 3
     ins, outs, held = refs[:count], refs[count : 2 * count], refs[2 * count : 3 * count]
     in_sem, out_sem = refs[3 * count :]
-    moves = []
-    for n in range(count):
-        size = ins[n].shape[0]
-        pieces = 4 if size % 64 == 0 and ins[n].dtype == jnp.bfloat16 else 1
-        step = size // pieces
-        for part in range(pieces):
-            rows = pl.ds(part * step, step)
-            moves.append((ins[n].at[rows], held[n].at[rows], outs[n].at[rows]))
-    first = [pltpu.make_async_copy(a, b, in_sem.at[m]) for m, (a, b, _) in enumerate(moves)]
-    second = [pltpu.make_async_copy(b, c, out_sem.at[m]) for m, (_, b, c) in enumerate(moves)]
+    first = [pltpu.make_async_copy(ins[n], held[n], in_sem.at[n]) for n in range(count)]
+    second = [pltpu.make_async_copy(held[n], outs[n], out_sem.at[n]) for n in range(count)]
     for copy in first:
         copy.start()
-    for m in range(len(moves)):
-        first[m].wait()
-        second[m].start()
+    for n in range(count):
+        first[n].wait()
+        second[n].start()
     for copy in second:
         copy.wait()
 
@@ -573,7 +564,7 @@
         out_shape=shapes,
         in_specs=[hbm] * len(shapes),
         out_specs=(hbm,) * len(shapes),
-        scratch_shapes=[pltpu.VMEM(a.shape, a.dtype) for a in shapes] + [dma((16,))] * 2,
+        scratch_shapes=[pltpu.VMEM(a.shape, a.dtype) for a in shapes] + [dma((len(shapes),))] * 2,
         compiler_params=pltpu.CompilerParams(vmem_limit_bytes=LIMIT),
     )(*results)
 

time: 48.9 us -> 46.3 us (0.947)
  Pallas kernels: 48.1 us -> 45.5 us
    pallas_call x1, Pallas kernels: 45.5 us -> 42.9 us  [fused(): pl.pallas_call(kernel, out_shape=shapes, in_specs=[hbm] * len(args), out_...]
where the time goes in v6:
time: 46.3 us; the launch traced here: 46.1 us
  Pallas kernels  45.5 us (98%)
  between operations  0.64 us (1%)
    pallas_call x1, Pallas kernels, fused(): pl.pallas_call(kernel, out_shape=shapes, in_specs=[hbm] * len(args), out_...  42.9 us
    pallas_call x1, Pallas kernels, fused(): pl.pallas_call(write_out, out_shape=shapes, in_specs=[hbm] * len(shapes),...  2.56 us

profile of v6, /device:TPU:0, one launch (start us, length us, event | category | flops | bytes accessed | tf_op | source)
XLA Modules:
  0.0 46.1 jit_solution(2422793969503189285)
XLA Ops:
  0.6 42.9 %shard_map.127 = (bf16[12,49,512]{2,1,0:T(8,128)(2,1)}, f32[64,256]{1,0:T(8,128)}, f32[64,256]{1,0:T(8,128)}, bf16[512,1024]{1,0:T(8,128)(2,1)}, f32[2,1024]{1,0:T(2,128)}, /*index=5*/f32[2,1024]{1,0:T(2,128)}) custom-call(bf16[12,49,512]{2,1,0:T(8,128)(2,1)} %act_hbm.1, bf16[12,49,1024]{2,1,0:T(8,128)(2,1)} %pre_hbm.1, f32[12,1024]{1,0:T(8,128)} %pool_hbm.1, ...), custom_call_target="tpu_custom_call" | custom-call | flops 1849688064 | bytes 8388608 | tf_op jit(solution)/shard_map/pallas_call | solution.py:526
  43.5 2.6 %shard_map.128 = (bf16[12,49,512]{2,1,0:T(8,128)(2,1)}, f32[64,256]{1,0:T(8,128)}, f32[64,256]{1,0:T(8,128)}, bf16[512,1024]{1,0:T(8,128)(2,1)}, f32[2,1024]{1,0:T(2,128)}, /*index=5*/f32[2,1024]{1,0:T(2,128)}) custom-call(bf16[12,49,512]{2,1,0:T(8,128)(2,1)} %get-tuple-element.12.refs_0_, f32[64,256]{1,0:T(8,128)} %get-tuple-element.13.refs_1_, ...), custom_call_target="tpu_custom_call" | custom-call | tf_op jit(solution)/shard_map/pallas_call | solution.py:562

commit v7 on v6

--- a/solution.py
+++ b/solution.py
@@ -299,9 +299,9 @@
     turned = a_s[...].T
     for q in range(n_row):
         at[q % 2, (q // 2) * rblk : (q // 2 + 1) * rblk, :] = turned[q * rblk : (q + 1) * rblk, :]
-    base_out()
     for copy in stats:
         copy.wait_recv()
+    base_out()
     parts = [jnp.concatenate([st[i, part] for part in range(n_col)], axis=1) for i in range(n_col)]
     mu = (parts[0][0:1] + parts[1][0:1] + parts[2][0:1] + parts[3][0:1]) / count
     square = parts[0][1:2] + parts[1][1:2] + parts[2][1:2] + parts[3][1:2]

time: 46.3 us -> 47.8 us (1.032)
  Pallas kernels: 45.5 us -> 47 us
    pallas_call x1, Pallas kernels: 42.9 us -> 44.4 us  [fused(): pl.pallas_call(kernel, out_shape=shapes, in_specs=[hbm] * len(args), out_...]
where the time goes in v7:
time: 47.8 us; the launch traced here: 47.6 us
  Pallas kernels  47 us (98%)
  between operations  0.64 us (1%)
    pallas_call x1, Pallas kernels, fused(): pl.pallas_call(kernel, out_shape=shapes, in_specs=[hbm] * len(args), out_...  44.4 us
    pallas_call x1, Pallas kernels, fused(): pl.pallas_call(write_out, out_shape=shapes, in_specs=[hbm] * len(shapes),...  2.56 us

profile of v7, /device:TPU:0, one launch (start us, length us, event | category | flops | bytes accessed | tf_op | source)
XLA Modules:
  0.0 47.6 jit_solution(4138992789925913536)
XLA Ops:
  0.6 44.4 %shard_map.127 = (bf16[12,49,512]{2,1,0:T(8,128)(2,1)}, f32[64,256]{1,0:T(8,128)}, f32[64,256]{1,0:T(8,128)}, bf16[512,1024]{1,0:T(8,128)(2,1)}, f32[2,1024]{1,0:T(2,128)}, /*index=5*/f32[2,1024]{1,0:T(2,128)}) custom-call(bf16[12,49,512]{2,1,0:T(8,128)(2,1)} %act_hbm.1, bf16[12,49,1024]{2,1,0:T(8,128)(2,1)} %pre_hbm.1, f32[12,1024]{1,0:T(8,128)} %pool_hbm.1, ...), custom_call_target="tpu_custom_call" | custom-call | flops 1849688064 | bytes 8388608 | tf_op jit(solution)/shard_map/pallas_call | solution.py:526
  45.0 2.6 %shard_map.128 = (bf16[12,49,512]{2,1,0:T(8,128)(2,1)}, f32[64,256]{1,0:T(8,128)}, f32[64,256]{1,0:T(8,128)}, bf16[512,1024]{1,0:T(8,128)(2,1)}, f32[2,1024]{1,0:T(2,128)}, /*index=5*/f32[2,1024]{1,0:T(2,128)}) custom-call(bf16[12,49,512]{2,1,0:T(8,128)(2,1)} %get-tuple-element.12.refs_0_, f32[64,256]{1,0:T(8,128)} %get-tuple-element.13.refs_1_, ...), custom_call_target="tpu_custom_call" | custom-call | tf_op jit(solution)/shard_map/pallas_call | solution.py:562
